TPU v7x, 256 devices: a whole 4x4x8 slice. The times are simulated.
256 devices in a mesh: tm: 32 (over y_lo, z, core), mp: 8 (over x, y_hi).
Axes of the slice: x: 4, y: 4 (y_hi: 2, y_lo: 2; y = y_hi * 2 + y_lo), z: 8, core: 2. Of those that a mesh axis runs over, the one named last changes fastest.
Arguments:
- queries: bfloat16 [4096, 6144], P('tm', 'mp'), may hold values from -13.5 to 13.5
- keys: bfloat16 [4096, 6144], P('tm', 'mp'), may hold values from -13.5 to 13.5
- values: bfloat16 [4096, 6144], P('tm', 'mp'), may hold values from -6 to 6
- window: int32 [32], P('tm'), may hold values from 0 to 4, as said below
- counts: int32 [32], P('tm'), may hold values from 32 to 128, as said below
- gain: float32 [6144], P('mp'), may hold values from 0.5 to 1.5
- w_gate: bfloat16 [6144, 16384], P('mp', 'tm'), may hold values from -0.078125 to 0.078125
- w_up: bfloat16 [6144, 16384], P('mp', 'tm'), may hold values from -0.078125 to 0.078125
- w_down: bfloat16 [16384, 6144], P('tm', 'mp'), may hold values from -0.046875 to 0.046875
Outputs:
- block_out: bfloat16 [4096, 6144], P('tm', 'mp')
Inputs may be any that keep to these rules, and one draw needn't show every extreme that they name: window[c] counts the prior groups group c sees; some group has 4. Group c's valid tokens fill its first counts[c] slots; some group is full.
All inputs are finite; a program needn't handle non-finite values.
Results may differ from a plain program's by a relative error of at most 0.025.
Values may be sent and summed in bfloat16 or wider, within the bound.
A program may use at most 128 MiB of HBM per device.

v0:
```python
import jax
import jax.numpy as jnp
from jax import lax
from jax.sharding import PartitionSpec as P

HD = 128
D = 6144
WMAX = 4


def shifted(value, axis, steps):
    count = lax.axis_size(axis)
    initial, last = (max(0, -steps), min(count, count - steps))
    return lax.ppermute(value, axis, [(source, source + steps) for source in range(initial, last)])


def per_device(queries, keys, values, window, counts, gain, w_gate, w_up, w_down):
    tok_rows = queries.shape[0]
    local_width = queries.shape[1]
    heads_here = local_width // HD
    group_index = lax.axis_index("tm")
    slots = jnp.arange(tok_rows, dtype=jnp.int32)
    received = []
    for offset in range(1, WMAX + 1):
        received.append(shifted((keys, values, counts), "tm", offset))
    key_list = [keys]
    value_list = [values]
    mask_list = [slots < counts[0]]
    for offset in range(1, WMAX + 1):
        far_keys, far_values, far_count = received[offset - 1]
        allowed = (offset <= window[0]) & (group_index - offset >= 0)
        key_list.append(far_keys)
        value_list.append(far_values)
        mask_list.append(allowed & (slots < far_count[0]))
    all_keys = jnp.concatenate(key_list, 0).reshape(-1, heads_here, HD)
    all_values = jnp.concatenate(value_list, 0).reshape(-1, heads_here, HD)
    visible = jnp.concatenate(mask_list, 0)
    query_heads = queries.reshape(tok_rows, heads_here, HD)
    scores = jnp.einsum(
        "qhd,khd->hqk", query_heads, all_keys, preferred_element_type=jnp.float32
    ) * HD ** (-0.5)
    scores = jnp.where(visible[None, None, :], scores, -1e30)
    top = jnp.max(scores, axis=-1, keepdims=True)
    expo = jnp.exp(scores - top)
    probs = (expo / jnp.sum(expo, axis=-1, keepdims=True)).astype(jnp.bfloat16)
    attended = jnp.einsum("hqk,khd->qhd", probs, all_values, preferred_element_type=jnp.float32)
    attended = attended.reshape(tok_rows, local_width)
    squares = lax.psum(jnp.sum(attended * attended, axis=1), "mp")
    normed = (attended * lax.rsqrt(squares[:, None] / D + 1e-06) * gain[None, :]).astype(
        jnp.bfloat16
    )
    hidden_here = w_gate.shape[1]
    both = jnp.concatenate([w_gate, w_up], 1)
    partial_sums = jnp.dot(
        lax.all_gather(normed, "tm", axis=0, tiled=True), both, preferred_element_type=jnp.float32
    )
    gate_share = lax.psum_scatter(
        partial_sums.astype(jnp.bfloat16), "mp", scatter_dimension=0, tiled=True
    ).astype(jnp.float32)
    hidden_share = (jax.nn.silu(gate_share[:, :hidden_here]) * gate_share[:, hidden_here:]).astype(
        jnp.bfloat16
    )
    hidden = lax.all_gather(hidden_share, "mp", axis=0, tiled=True)
    ffn = lax.psum_scatter(
        jnp.dot(hidden, w_down, preferred_element_type=jnp.float32).astype(jnp.bfloat16),
        "tm",
        scatter_dimension=0,
        tiled=True,
    ).astype(jnp.float32)
    return (normed.astype(jnp.float32) + ffn).astype(jnp.bfloat16)


def solution(mesh):
    in_specs = (
        P("tm", "mp"),
        P("tm", "mp"),
        P("tm", "mp"),
        P("tm"),
        P("tm"),
        P("mp"),
        P("mp", "tm"),
        P("mp", "tm"),
        P("tm", "mp"),
    )
    out_specs = P("tm", "mp")
    return jax.shard_map(
        per_device, mesh=mesh, in_specs=in_specs, out_specs=out_specs, check_vma=False
    )
```

profile of v0, /device:TPU:1, one launch (start us, length us, event | category | flops | bytes accessed | tf_op | source)
XLA Modules:
  0.0 521.0 jit_solution(763776466552942941)
XLA Ops:
  6.5 5.1 collective-permute-start.5
  11.6 3.8 collective-permute-start.4
  15.4 6.7 %collective-permute-start.7 = (s32[1]{0:T(128)}, s32[1]{0:T(128)}, u32[]{:S(2)}, u32[]{:S(2)}) collective-permute-start(s32[1]{0:T(128)} %param.13), channel_id=1, source_target_pairs={{0,32},{8,40},{16,48},{24,56},{32,64},{40,72},{48,80},{56,88},{64,... | collective-permute-start | bytes 20 | tf_op jit(solution)/shard_map/ppermute | solution.py:14
  22.1 2.7 collective-permute-start.6
  24.8 1.1 copy.19
  25.9 2.5 collective-permute-start.11
  29.1 0.7 constant_dynamic-update-slice_fusion.9
  30.5 1.1 copy.20
  31.6 0.9 constant_dynamic-update-slice_fusion.4
  32.5 0.2 dynamic-update-slice.5
  32.8 0.0 collective-permute-done.5
  32.8 2.5 collective-permute-start.10
  35.2 0.6 compare_and_fusion.2
  35.9 0.0 collective-permute-done.4
  35.9 3.7 collective-permute-start.9
  39.6 0.6 compare_and_fusion.3
  40.2 0.2 dynamic-update-slice.6
  40.4 0.2 dynamic-update-slice.7
  40.6 0.0 collective-permute-done.6
  40.6 1.9 collective-permute-start
  42.6 0.7 compare_and_fusion.1
  43.3 0.2 dynamic-update-slice.8
  43.5 0.0 collective-permute-done.7
  43.5 3.2 collective-permute-start.1
  46.7 0.6 compare_and_fusion
  47.3 0.2 dynamic-update-slice.9
  47.5 5.4 %collective-permute-done = bf16[128,768]{1,0:T(8,128)(2,1)S(1)} collective-permute-done((bf16[128,768]{1,0:T(8,128)(2,1)}, bf16[128,768]{1,0:T(8,128)(2,1)S(1)}, u32[]{:S(2)}, u32[]{:S(2)}) %collective-permute-start) | collective-permute-done | bytes 196640 | tf_op jit(solution)/shard_map/ppermute | solution.py:14
  52.9 1.3 collective-permute-start.2
  54.3 2.2 collective-permute-done.1
  56.5 2.2 collective-permute-start.3
  58.7 4.6 collective-permute-done.2
  63.3 1.9 collective-permute-start.8
  65.2 1.4 collective-permute-done.3
  66.6 0.6 copy.14
  67.2 2.2 collective-permute-done.8
  69.4 1.6 constant_dynamic-update-slice_fusion.8
  71.0 0.0 collective-permute-done.9
  71.0 1.6 constant_dynamic-update-slice_fusion.7
  72.7 0.0 collective-permute-done.10
  72.7 0.7 constant_dynamic-update-slice_fusion.6
  73.4 0.0 collective-permute-done.11
  73.4 0.7 constant_dynamic-update-slice_fusion.5
  74.1 3.4 fusion.19
  77.5 2.0 fusion.13
  79.5 23.1 %psum.7 = f32[128]{0:T(128)S(1)} all-reduce(f32[128]{0:T(128)S(1)} %get-tuple-element.7), channel_id=1, replica_groups=mesh['tm'=32,'mp'=8] {'mp'}, use_global_device_ids=true, to_apply=%region_3.4 | all-reduce | flops 128 | bytes 1024 | tf_op jit(solution)/shard_map/psum | solution.py:48
  102.7 0.2 copy.24
  102.8 0.8 multiply_convert_fusion
  103.6 0.0 all-gather.3.cloned.1.call-update
  103.6 0.0 reduce-scatter.3.cloned.1.call-start
  103.7 73.1 %all-gather.3.cloned.1.call-done = bf16[4096,768]{1,0:T(8,128)(2,1)} async-done(((bf16[128,768]{1,0:T(8,128)(2,1)}), bf16[4096,768]{1,0:T(8,128)(2,1)}) %all-gather.3.cloned.1.call-update) | async-done | bytes 6291472 | tf_op jit(solution)/shard_map/all_gather | solution.py:55
  176.7 0.0 copy-done.2
  176.7 10.9 %convolution_convert_fusion = bf16[4096,1024]{1,0:T(8,128)(2,1)} fusion(bf16[4096,768]{1,0:T(8,128)(2,1)} %all-gather.3.cloned.1.call-done, bf16[768,512]{1,0:T(8,128)(2,1)S(1)} %copy-done.2, bf16[768,512]{1,0:T(8,128)(2,1)} %param.15), kind=kOutput, calls=%fused_computation.1 | convolution fusion | flops 6449790976 | bytes 16252928 | tf_op jit(solution)/shard_map/dot_general | solution.py:54
  187.7 0.0 reduce-scatter.3.cloned.1.call-update
  187.7 0.0 all-gather.5.cloned.1.call-start
  187.7 119.1 %reduce-scatter.3.cloned.1.call-done = bf16[512,1024]{1,0:T(8,128)(2,1)} async-done(((bf16[4096,1024]{1,0:T(8,128)(2,1)}), bf16[512,1024]{1,0:T(8,128)(2,1)}) %reduce-scatter.3.cloned.1.call-update) | async-done | bytes 1048592 | tf_op jit(solution)/shard_map/reduce_scatter | solution.py:57
  306.8 1.5 convert_element_type.31
  308.3 1.1 fusion.8
  309.4 0.0 all-gather.5.cloned.1.call-update
  309.4 0.0 reduce-scatter.5.cloned.1.call-start
  309.5 74.8 %all-gather.5.cloned.1.call-done = bf16[4096,512]{1,0:T(8,128)(2,1)} async-done(((bf16[512,512]{1,0:T(8,128)(2,1)}), bf16[4096,512]{1,0:T(8,128)(2,1)}) %all-gather.5.cloned.1.call-update) | async-done | bytes 4194320 | tf_op jit(solution)/shard_map/all_gather | solution.py:63
  384.2 8.3 %convolution_convert_fusion.1 = bf16[4096,768]{1,0:T(8,128)(2,1)} fusion(bf16[4096,512]{1,0:T(8,128)(2,1)} %all-gather.5.cloned.1.call-done, bf16[512,768]{1,0:T(8,128)(2,1)S(1)} %copy-done), kind=kOutput, calls=%fused_computation.2 | convolution fusion | flops 3224371200 | bytes 11272192 | tf_op jit(solution)/shard_map/dot_general | solution.py:65
  392.5 0.0 reduce-scatter.5.cloned.1.call-update
  392.5 120.2 %reduce-scatter.5.cloned.1.call-done = bf16[128,768]{1,0:T(8,128)(2,1)} async-done(((bf16[4096,768]{1,0:T(8,128)(2,1)}), bf16[128,768]{1,0:T(8,128)(2,1)}) %reduce-scatter.5.cloned.1.call-update) | async-done | bytes 196624 | tf_op jit(solution)/shard_map/reduce_scatter | solution.py:64
  512.8 1.7 add_convert_fusion
  (13 shorter events, 0.1 us)
Async XLA Ops:
  6.5 377.7 %copy-start = (bf16[512,768]{1,0:T(8,128)(2,1)S(1)}, bf16[512,768]{1,0:T(8,128)(2,1)}, u32[]{:S(2)}) copy-start(bf16[512,768]{1,0:T(8,128)(2,1)} %param.17) | copy-start | bytes 2359300
  6.5 170.2 %all-gather.3.cloned.1.call-start = ((), (), s32[]{:S(2)}) async-start(), calls=%async_computation.2 | async-start | bytes 6488064 | tf_op jit(solution)/shard_map/all_gather | solution.py:55
  6.5 26.2 %collective-permute-start.5 = (s32[1]{0:T(128)}, s32[1]{0:T(128)}, u32[]{:S(2)}, u32[]{:S(2)}) collective-permute-start(s32[1]{0:T(128)} %param.13), channel_id=1, source_target_pairs={{0,16},{8,24},{16,32},{24,40},{32,48},{40,56},{48,64},{56,72},{64,... | collective-permute-start | bytes 20 | tf_op jit(solution)/shard_map/ppermute | solution.py:14
  11.6 24.3 %collective-permute-start.4 = (s32[1]{0:T(128)}, s32[1]{0:T(128)}, u32[]{:S(2)}, u32[]{:S(2)}) collective-permute-start(s32[1]{0:T(128)} %param.13), channel_id=1, source_target_pairs={{0,8},{8,16},{16,24},{24,32},{32,40},{40,48},{48,56},{56,64},{64,7... | collective-permute-start | bytes 20 | tf_op jit(solution)/shard_map/ppermute | solution.py:14
  15.4 28.0 %collective-permute-start.7 = (s32[1]{0:T(128)}, s32[1]{0:T(128)}, u32[]{:S(2)}, u32[]{:S(2)}) collective-permute-start(s32[1]{0:T(128)} %param.13), channel_id=1, source_target_pairs={{0,32},{8,40},{16,48},{24,56},{32,64},{40,72},{48,80},{56,88},{64,... | collective-permute-start | bytes 20 | tf_op jit(solution)/shard_map/ppermute | solution.py:14
  22.1 18.5 %collective-permute-start.6 = (s32[1]{0:T(128)}, s32[1]{0:T(128)}, u32[]{:S(2)}, u32[]{:S(2)}) collective-permute-start(s32[1]{0:T(128)} %param.13), channel_id=1, source_target_pairs={{0,24},{8,32},{16,40},{24,48},{32,56},{40,64},{48,72},{56,80},{64,... | collective-permute-start | bytes 20 | tf_op jit(solution)/shard_map/ppermute | solution.py:14
  25.9 47.5 %collective-permute-start.11 = (bf16[128,768]{0,1:T(8,128)(2,1)S(1)}, bf16[128,768]{0,1:T(8,128)(2,1)S(1)}, u32[]{:S(2)}, u32[]{:S(2)}) collective-permute-start(bf16[128,768]{0,1:T(8,128)(2,1)S(1)} %copy.19), channel_id=1, source_target_pairs={{0,32},{8,40},{16,48},{24,56},{32,64},{40,72},{48,80},{56,88},{64,... | collective-permute-start | bytes 589832 | tf_op jit(solution)/shard_map/ppermute | solution.py:14
  32.8 39.9 %collective-permute-start.10 = (bf16[128,768]{0,1:T(8,128)(2,1)S(1)}, bf16[128,768]{0,1:T(8,128)(2,1)S(1)}, u32[]{:S(2)}, u32[]{:S(2)}) collective-permute-start(bf16[128,768]{0,1:T(8,128)(2,1)S(1)} %copy.19), channel_id=1, source_target_pairs={{0,24},{8,32},{16,40},{24,48},{32,56},{40,64},{48,72},{56,80},{64,... | collective-permute-start | bytes 589832 | tf_op jit(solution)/shard_map/ppermute | solution.py:14
  35.9 35.2 %collective-permute-start.9 = (bf16[128,768]{0,1:T(8,128)(2,1)S(1)}, bf16[128,768]{0,1:T(8,128)(2,1)}, u32[]{:S(2)}, u32[]{:S(2)}) collective-permute-start(bf16[128,768]{0,1:T(8,128)(2,1)S(1)} %copy.19), channel_id=1, source_target_pairs={{0,16},{8,24},{16,32},{24,40},{32,48},{40,56},{48,64},{56,72},{64,... | collective-permute-start | bytes 589832 | tf_op jit(solution)/shard_map/ppermute | solution.py:14
  40.6 12.3 %collective-permute-start = (bf16[128,768]{1,0:T(8,128)(2,1)}, bf16[128,768]{1,0:T(8,128)(2,1)S(1)}, u32[]{:S(2)}, u32[]{:S(2)}) collective-permute-start(bf16[128,768]{1,0:T(8,128)(2,1)} %param.11), channel_id=1, source_target_pairs={{0,8},{8,16},{16,24},{24,32},{32,40},{40,48},{48,56},{56,64},{64,7... | collective-permute-start | bytes 589832 | tf_op jit(solution)/shard_map/ppermute | solution.py:14
  43.5 13.0 %collective-permute-start.1 = (bf16[128,768]{1,0:T(8,128)(2,1)}, bf16[128,768]{1,0:T(8,128)(2,1)S(1)}, u32[]{:S(2)}, u32[]{:S(2)}) collective-permute-start(bf16[128,768]{1,0:T(8,128)(2,1)} %param.11), channel_id=1, source_target_pairs={{0,16},{8,24},{16,32},{24,40},{32,48},{40,56},{48,64},{56,72},{64,... | collective-permute-start | bytes 589832 | tf_op jit(solution)/shard_map/ppermute | solution.py:14
  52.9 10.3 %collective-permute-start.2 = (bf16[128,768]{1,0:T(8,128)(2,1)}, bf16[128,768]{1,0:T(8,128)(2,1)S(1)}, u32[]{:S(2)}, u32[]{:S(2)}) collective-permute-start(bf16[128,768]{1,0:T(8,128)(2,1)} %param.11), channel_id=1, source_target_pairs={{0,24},{8,32},{16,40},{24,48},{32,56},{40,64},{48,72},{56,80},{64,... | collective-permute-start | bytes 589832 | tf_op jit(solution)/shard_map/ppermute | solution.py:14
  56.5 10.1 %collective-permute-start.3 = (bf16[128,768]{1,0:T(8,128)(2,1)}, bf16[128,768]{1,0:T(8,128)(2,1)S(1)}, u32[]{:S(2)}, u32[]{:S(2)}) collective-permute-start(bf16[128,768]{1,0:T(8,128)(2,1)} %param.11), channel_id=1, source_target_pairs={{0,32},{8,40},{16,48},{24,56},{32,64},{40,72},{48,80},{56,88},{64,... | collective-permute-start | bytes 589832 | tf_op jit(solution)/shard_map/ppermute | solution.py:14
  63.3 6.1 %collective-permute-start.8 = (bf16[128,768]{0,1:T(8,128)(2,1)S(1)}, bf16[128,768]{0,1:T(8,128)(2,1)}, u32[]{:S(2)}, u32[]{:S(2)}) collective-permute-start(bf16[128,768]{0,1:T(8,128)(2,1)S(1)} %copy.19), channel_id=1, source_target_pairs={{0,8},{8,16},{16,24},{24,32},{32,40},{40,48},{48,56},{56,64},{64,7... | collective-permute-start | bytes 589832 | tf_op jit(solution)/shard_map/ppermute | solution.py:14
  77.5 25.3 %copy-start.1 = (f32[768]{0:T(1024)S(1)}, f32[768]{0:T(1024)}, u32[]{:S(2)}) copy-start(f32[768]{0:T(1024)} %param.14) | copy-start | bytes 9220
  77.5 99.3 %copy-start.2 = (bf16[768,512]{1,0:T(8,128)(2,1)S(1)}, bf16[768,512]{1,0:T(8,128)(2,1)}, u32[]{:S(2)}) copy-start(bf16[768,512]{1,0:T(8,128)(2,1)} %param.16) | copy-start | bytes 2359300
  103.6 203.2 %reduce-scatter.3.cloned.1.call-start = ((), (), s32[]{:S(2)}) async-start(), calls=%async_computation.3 | async-start | bytes 9437184 | tf_op jit(solution)/shard_map/reduce_scatter | solution.py:57
  187.7 196.5 %all-gather.5.cloned.1.call-start = ((), (), s32[]{:S(2)}) async-start(), calls=%async_computation.4 | async-start | bytes 4718592 | tf_op jit(solution)/shard_map/all_gather | solution.py:63
  309.4 203.4 %reduce-scatter.5.cloned.1.call-start = ((), (), s32[]{:S(2)}) async-start(), calls=%async_computation.5 | async-start | bytes 6488064 | tf_op jit(solution)/shard_map/reduce_scatter | solution.py:64
Sparse Core Ops, SparseCore 0:
  103.8 72.9 all-gather.2
  187.8 118.9 reduce-scatter.2
  309.5 74.6 all-gather.4
  392.7 120.0 reduce-scatter.4
where the time goes:
time: 525 us; the launch traced here: 521 us
  waiting for transfers between devices  403 us (77%)
  starting transfers between devices  37.5 us (7%)
  matrix products  24.7 us (5%)
  blocking collectives  23.1 us (4%)
  between operations  14.7 us (3%)
  local copies, waits for them, and re-layouts  10.5 us (2%)
  other arithmetic  7.66 us (1%)
    reduce_scatter x1, waiting for transfers between devices, per_device(): lax.psum_scatter(jnp.dot(hidden, w_down, preferred_element_type=jnp.float...  120 us
    reduce_scatter x1, waiting for transfers between devices, per_device(): lax.psum_scatter(partial_sums.astype(jnp.bfloat16), 'mp', scatter_dimensi...  119 us
    all_gather x1, waiting for transfers between devices, per_device(): hidden = lax.all_gather(hidden_share, 'mp', axis=0, tiled=True)  74.8 us
    all_gather x1, waiting for transfers between devices, per_device(): lax.all_gather(normed, 'tm', axis=0, tiled=True)  73.1 us
    ppermute x12, starting transfers between devices, shifted(): lax.ppermute(value, axis, [(source, source + steps) for source in range(i...  37.4 us
    psum x1, blocking collectives, per_device(): squares = lax.psum(jnp.sum(attended * attended, axis=1), 'mp')  23.1 us
    ppermute x12, waiting for transfers between devices, shifted(): lax.ppermute(value, axis, [(source, source + steps) for source in range(i...  15.8 us
    dot_general x1, matrix products, per_device(): jnp.dot(lax.all_gather(normed, 'tm', axis=0, tiled=True), both, preferred...  10.9 us
  transfers between devices with their start and end apart: 16, of which 9 were waited for; matrix products, arithmetic and copies ran while one was open for 2% of the time, Pallas kernels for 0%

commit v1 on v0

v1 whole, which is shorter than its diff:
```python
import functools

import jax
import jax.numpy as jnp
from jax import lax
from jax.experimental import pallas as pl
from jax.experimental.pallas import tpu as pltpu
from jax.sharding import PartitionSpec as P

MESH = pl.DeviceIdType.MESH
HD = 128
D = 6144
WMAX = 4
TOK = 128
HALF = 64
WID = 768
HID = 512
NX = 4
NZ = 8
SPLITS = ((0, 32), (32, 32))
SLOT = {0: 0, 1: 1, -1: 2, 2: 3, -2: 4, 3: 5, -3: 6, 4: 7}
GROUPS = ((0, 1), (1, 2), (3, 2), (5, 2), (7, 1))


def body(
    q_hbm, k_hbm, v_hbm, win_ref, cnt_ref, gain_ref, wg_hbm, wu_hbm, wd_hbm, out_ref, *scratch
):
    (q_ref, k_ref, v_ref, cn_ref, s_ref, att_ref, ss_ref, nrm_ref, wgu_ref, wd_ref) = scratch[:10]
    (x_refs, ps_refs, pr_refs, h_refs, os_refs, oc_refs, oo_refs, rs_refs, rr_refs, f_refs) = scratch[10:20]
    (load_sem, kv_send, kv_recv, w_send, w_recv, ss_send, ss_recv) = scratch[20:27]
    (y_sem, ag_sem, rl_sem, p_sem, h_sem, o_sem, r_sem, f_sem) = scratch[27:35]

    tm = lax.axis_index("tm")
    mp = lax.axis_index("mp")
    yl, z, c = tm // 16, (tm // 2) % NZ, tm % 2
    x, yh = mp // 2, mp % 2

    def dev(yl_=yl, z_=z, c_=c, x_=x, yh_=yh):
        return (yl_ * 16 + z_ * 2 + c_, x_ * 2 + yh_)

    z_up, z_down = lax.rem(z + 1, NZ), lax.rem(z + NZ - 1, NZ)
    core = dev(c_=1 - c)
    y_l, y_h, y_lh = dev(yl_=1 - yl), dev(yh_=1 - yh), dev(yl_=1 - yl, yh_=1 - yh)
    ups = (dev(z_=z_up), dev(z_=z_down))
    xs = [lax.rem(x + j, NX) for j in range(NX)]
    x_dev = [dev(x_=xs[j]) for j in range(NX)]
    xh_dev = [dev(x_=xs[j], yh_=1 - yh) for j in range(NX)]
    next_chip = (lax.rem(tm + 2, 32), mp)
    prev_chip = (lax.rem(tm + 30, 32), mp)

    sent = []

    def remote(src, dst, send_sem, recv_sem, device):
        copy = pltpu.make_async_remote_copy(
            src_ref=src, dst_ref=dst, send_sem=send_sem, recv_sem=recv_sem,
            device_id=device, device_id_type=MESH,
        )
        copy.start()
        sent.append(copy)
        return copy

    loads = []
    for i, (src, dst) in enumerate((
        (k_hbm, k_ref.at[0]), (v_hbm, v_ref.at[0]), (q_hbm, q_ref),
        (wg_hbm, wgu_ref.at[0, :, pl.ds(0, HID)]), (wu_hbm, wgu_ref.at[0, :, pl.ds(HID, HID)]),
        (wd_hbm, wd_ref.at[0]),
    )):
        copy = pltpu.make_async_copy(src, dst, load_sem.at[i])
        copy.start()
        loads.append(copy)

    cn_ref[0] = jnp.full((8, 128), cnt_ref[0], jnp.int32)

    barrier = pltpu.get_barrier_semaphore()
    partners = (core, y_l, y_h, y_lh, *ups, *x_dev[1:], *xh_dev[1:], next_chip, prev_chip)
    for device in partners:
        pl.semaphore_signal(barrier, inc=1, device_id=device, device_id_type=MESH)
    pl.semaphore_wait(barrier, len(partners))

    kv = (cn_ref, k_ref, v_ref)

    def kv_copy(i, src, dst, sem, device):
        return remote(kv[i].at[src], kv[i].at[dst], kv_send.at[sem, i], kv_recv.at[sem, i], device)

    loads[0].wait()
    loads[1].wait()
    own = [kv_copy(i, 0, 2, 0, next_chip) for i in range(3)]
    w_copies = [
        remote(wg_hbm, wgu_ref.at[1, :, pl.ds(0, HID)], w_send.at[0], w_recv.at[0], y_h),
        remote(wu_hbm, wgu_ref.at[1, :, pl.ds(HID, HID)], w_send.at[1], w_recv.at[1], y_h),
        remote(wd_hbm, wd_ref.at[1], w_send.at[2], w_recv.at[2], y_h),
    ]
    loads[2].wait()

    keys_at = lax.broadcasted_iota(jnp.int32, (1, TOK), 1)
    window = jnp.full((1, TOK), win_ref[0], jnp.int32)
    place = jnp.full((1, TOK), tm, jnp.int32)

    def score(e):
        visible = keys_at < cn_ref[e, 0:1, :]
        if e > 0:
            visible = visible & (window >= e) & (place >= e)
        for h in range(WID // HD):
            cols = pl.ds(h * HD, HD)
            s = lax.dot_general(
                q_ref[:, cols], k_ref[e, :, cols], (((1,), (1,)), ((), ())),
                preferred_element_type=jnp.float32,
            ) * HD ** (-0.5)
            s_ref[h, :, pl.ds(e * TOK, TOK)] = jnp.where(visible, s, -1e30)

    score(0)
    far, near, mid = [], [], []
    for i in range(3):
        own[i].wait_recv()
        far.append(kv_copy(i, 2, 4, 1, next_chip))
        near.append(kv_copy(i, 2 * c, 1, 2, core))
    score(2)
    for i in range(3):
        near[i].wait_recv()
    score(1)
    for i in range(3):
        far[i].wait_recv()
        mid.append(kv_copy(i, 2 * c + 2, 3, 3, core))
    score(4)
    for i in range(3):
        mid[i].wait_recv()
    score(3)

    squares = jnp.zeros((TOK, HD), jnp.float32)
    for h in range(WID // HD):
        cols = pl.ds(h * HD, HD)
        s = s_ref[h]
        expo = jnp.exp(s - jnp.max(s, axis=-1, keepdims=True))
        total = jnp.sum(expo, axis=-1, keepdims=True)
        vals = v_ref[:, :, cols].reshape((WMAX + 1) * TOK, HD)
        att = jnp.dot(expo.astype(jnp.bfloat16), vals, preferred_element_type=jnp.float32) / total
        att_ref[:, cols] = att
        squares = squares + att * att
    row = jnp.broadcast_to(jnp.sum(squares, axis=1, keepdims=True), (TOK, TOK))
    ss_ref[0] = jnp.transpose(row)[0:8]
    ss_copies = [
        remote(ss_ref.at[0], ss_ref.at[j], ss_send.at[j], ss_recv.at[j], device)
        for j, device in enumerate((y_h, *x_dev[1:], *xh_dev[1:]), start=1)
    ]
    for copy in ss_copies:
        copy.wait_recv()
    total = ss_ref[0]
    for j in range(1, 8):
        total = total + ss_ref[j]
    factor = lax.rsqrt(total / D + 1e-06)
    factor = jnp.transpose(jnp.broadcast_to(factor[0:1], (TOK, TOK)))
    for h in range(WID // HD):
        cols = pl.ds(h * HD, HD)
        normed = (att_ref[:, cols] * factor * gain_ref[:, cols]).astype(jnp.bfloat16)
        nrm_ref[:, :, cols] = normed.reshape(2, HALF, HD)

    y_copies = []
    for i, (off, size) in enumerate(SPLITS):
        rows = pl.ds(off, size)
        x_refs[i][0, 0, 0, 0] = nrm_ref[yh, rows]
        y_copies.append([
            remote(nrm_ref.at[1 - yh, rows], x_refs[i].at[0, 0, 1, 0], y_sem.at[0, i, 0], y_sem.at[1, i, 0], y_h),
            remote(nrm_ref.at[yh, rows], x_refs[i].at[0, 0, 0, 1], y_sem.at[0, i, 1], y_sem.at[1, i, 1], y_l),
            remote(nrm_ref.at[1 - yh, rows], x_refs[i].at[0, 0, 1, 1], y_sem.at[0, i, 2], y_sem.at[1, i, 2], y_lh),
        ])

    ring, relay = {}, {}

    def ring_send(i, way, m):
        sign = (-1, 1)[way]
        src = 0 if m == 1 else SLOT[sign * (m - 1)]
        dst = SLOT[4 if m == 4 else sign * m]
        src_ref, dst_ref = x_refs[i].at[src, 0], x_refs[i].at[dst, 0]
        if m == 4:
            src_ref, dst_ref = src_ref.at[way], dst_ref.at[way]
        ring[i, way, m] = remote(
            src_ref, dst_ref, ag_sem.at[0, i, way, m - 1], ag_sem.at[1, i, way, m - 1], ups[way]
        )

    def relay_send(i, slot):
        relay[i, slot] = remote(
            x_refs[i].at[slot, 0], x_refs[i].at[slot, 1], rl_sem.at[0, i, slot], rl_sem.at[1, i, slot], core
        )

    def gather(i, m):
        if m == 0:
            for copy in y_copies[i]:
                copy.wait_recv()
            ring_send(i, 0, 1)
            ring_send(i, 1, 1)
            relay_send(i, 0)
            return
        for way in range(2):
            ring[i, way, m].wait_recv()
            if m < 4:
                ring_send(i, way, m + 1)
                relay_send(i, SLOT[(-1, 1)[way] * m])
        if m == 4:
            relay_send(i, SLOT[4])

    p_copies, h_copies, o_copies, r_copies, f_copies = {}, {}, {}, {}, {}

    def gate_up(i, m):
        slot, count = GROUPS[m]
        size = SPLITS[i][1]
        for k in range(slot, slot + count):
            relay[i, k].wait_recv()
        for n in range(0, 2 * HID, 256):
            acc = None
            for half in range(2):
                tokens = x_refs[i][slot : slot + count, :, half].reshape(count * 4 * size, WID)
                part = jnp.dot(tokens, wgu_ref[half, :, n : n + 256], preferred_element_type=jnp.float32)
                acc = part if acc is None else acc + part
            ps_refs[i][slot : slot + count, :, :, n : n + 256] = acc.astype(jnp.bfloat16).reshape(
                count, 4, size, 256
            )
        p_copies[i, m] = [
            remote(
                ps_refs[i].at[pl.ds(slot, count), xs[j]], pr_refs[i].at[pl.ds(slot, count), j - 1],
                p_sem.at[0, i, m, j - 1], p_sem.at[1, i, m, j - 1], x_dev[j],
            )
            for j in (2, 1, 3)
        ]

    def hidden(i, m):
        slot, count = GROUPS[m]
        for copy in p_copies[i, m]:
            copy.wait_recv()
        for k in range(slot, slot + count):
            both = ps_refs[i][k, x].astype(jnp.float32)
            for j in range(NX - 1):
                both = both + pr_refs[i][k, j].astype(jnp.float32)
            gate, up = both[:, :HID], both[:, HID:]
            h_refs[i][k, x] = (gate / (1.0 + jnp.exp(-gate)) * up).astype(jnp.bfloat16)
        ref = h_refs[i].at[pl.ds(slot, count), x]
        h_copies[i, m] = [
            remote(ref, ref, h_sem.at[0, i, m, j - 1], h_sem.at[1, i, m, j - 1], x_dev[j]) for j in (2, 1, 3)
        ]

    def down(i, m):
        slot, count = GROUPS[m]
        size = SPLITS[i][1]
        for copy in h_copies[i, m]:
            copy.wait_recv()
        rows = h_refs[i][slot : slot + count].reshape(count * 4 * size, HID)
        for half in range(2):
            for n in range(0, WID, 256):
                o = jnp.dot(rows, wd_ref[half, :, n : n + 256], preferred_element_type=jnp.float32)
                o = o.reshape(count, 2, 2, size, 256)
                oo_refs[i][slot : slot + count, half, :, :, n : n + 256] = o[:, 0]
                os_refs[i][slot : slot + count, half, :, :, n : n + 256] = o[:, 1].astype(jnp.bfloat16)
        o_copies[i, m] = remote(
            os_refs[i].at[pl.ds(slot, count)], oc_refs[i].at[pl.ds(slot, count)],
            o_sem.at[0, i, m], o_sem.at[1, i, m], core,
        )

    def both_cores(i, m):
        slot, count = GROUPS[m]
        o_copies[i, m].wait_recv()
        for k in range(slot, slot + count):
            oo_refs[i][k] += oc_refs[i][k].astype(jnp.float32)

    def sums(i, r):
        for way in range(2):
            sign = (1, -1)[way]
            if r == 0:
                rs_refs[i][way, 0, 0] = oo_refs[i][SLOT[4], way].astype(jnp.bfloat16)
                src, dst = rs_refs[i].at[way, 0, 0], rr_refs[i].at[way, 0, way]
            else:
                r_copies[i, way, r - 1].wait_recv()
                slot = SLOT[sign * (4 - r)]
                if r == 1:
                    rs_refs[i][way, 1, way] = (
                        oo_refs[i][slot, way] + rr_refs[i][way, 0, way].astype(jnp.float32)
                    ).astype(jnp.bfloat16)
                    rs_refs[i][way, 1, 1 - way] = oo_refs[i][slot, 1 - way].astype(jnp.bfloat16)
                else:
                    rs_refs[i][way, r] = (
                        oo_refs[i][slot] + rr_refs[i][way, r - 1].astype(jnp.float32)
                    ).astype(jnp.bfloat16)
                src, dst = rs_refs[i].at[way, r], rr_refs[i].at[way, r]
            r_copies[i, way, r] = remote(src, dst, r_sem.at[0, i, way, r], r_sem.at[1, i, way, r], ups[way])

    def deliver(i):
        for way in range(2):
            r_copies[i, way, 3].wait_recv()
        ref = oo_refs[i]
        own = rr_refs[i]
        ref[0] += own[0, 3].astype(jnp.float32) + own[1, 3].astype(jnp.float32)
        for j, (half, group, device) in enumerate(((0, 1, y_l), (1, 0, y_h), (1, 1, y_lh))):
            f_refs[i][0, j] = ref[0, half, group].astype(jnp.bfloat16)
            f_copies[i, j] = remote(
                f_refs[i].at[0, j], f_refs[i].at[1, j], f_sem.at[0, i, j], f_sem.at[1, i, j], device
            )

    def finish(i):
        off, size = SPLITS[i]
        rows = pl.ds(off, size)
        for j in range(3):
            f_copies[i, j].wait_recv()
        got = f_refs[i]
        mine = oo_refs[i][0, 0, 0] + got[1, 0].astype(jnp.float32)
        theirs = got[1, 1].astype(jnp.float32) + got[1, 2].astype(jnp.float32)
        out_ref[yh, rows] = (nrm_ref[yh, rows].astype(jnp.float32) + mine).astype(jnp.bfloat16)
        out_ref[1 - yh, rows] = (nrm_ref[1 - yh, rows].astype(jnp.float32) + theirs).astype(jnp.bfloat16)

    steps = [(i, m) for i in range(len(SPLITS)) for m in range(len(GROUPS))]
    for i in range(len(SPLITS)):
        gather(i, 0)
    for copy in loads[3:]:
        copy.wait()
    for copy in w_copies[:2]:
        copy.wait_recv()
    tail = []
    for k in range(len(steps) + 3):
        if k < len(steps):
            gate_up(*steps[k])
        if k + 1 < len(steps) and steps[k + 1][1] > 0:
            gather(*steps[k + 1])
        if 0 <= k - 1 < len(steps):
            hidden(*steps[k - 1])
        if 0 <= k - 2 < len(steps):
            if k == 2:
                w_copies[2].wait_recv()
            down(*steps[k - 2])
        if 0 <= k - 3 < len(steps):
            i, m = steps[k - 3]
            both_cores(i, m)
            if m == len(GROUPS) - 1:
                tail += [functools.partial(sums, i, r) for r in range(4)]
                tail += [functools.partial(deliver, i), functools.partial(finish, i)]
        if tail:
            tail.pop(0)()
    for part in tail:
        part()

    for copy in sent:
        copy.wait_send()


def per_device(queries, keys, values, window, counts, gain, w_gate, w_up, w_down):
    bf, f32 = jnp.bfloat16, jnp.float32
    n = len(SPLITS)
    sizes = [size for _, size in SPLITS]

    def each(shape_of, dtype):
        return [pltpu.VMEM(shape_of(size), dtype) for size in sizes]

    dma = pltpu.SemaphoreType.DMA
    steps = len(GROUPS)
    scratch = [
        pltpu.VMEM((TOK, WID), bf),
        pltpu.VMEM((WMAX + 1, TOK, WID), bf),
        pltpu.VMEM((WMAX + 1, TOK, WID), bf),
        pltpu.VMEM((WMAX + 1, 8, 128), jnp.int32),
        pltpu.VMEM((WID // HD, TOK, (WMAX + 1) * TOK), f32),
        pltpu.VMEM((TOK, WID), f32),
        pltpu.VMEM((8, 8, 128), f32),
        pltpu.VMEM((2, HALF, WID), bf),
        pltpu.VMEM((2, WID, 2 * HID), bf),
        pltpu.VMEM((2, HID, WID), bf),
        each(lambda s: (NZ, 2, 2, 2, s, WID), bf),
        each(lambda s: (NZ, NX, s, 2 * HID), bf),
        each(lambda s: (NZ, NX - 1, s, 2 * HID), bf),
        each(lambda s: (NZ, NX, s, HID), bf),
        each(lambda s: (NZ, 2, 2, s, WID), bf),
        each(lambda s: (NZ, 2, 2, s, WID), bf),
        each(lambda s: (NZ, 2, 2, s, WID), f32),
        each(lambda s: (2, 4, 2, 2, s, WID), bf),
        each(lambda s: (2, 4, 2, 2, s, WID), bf),
        each(lambda s: (2, 3, s, WID), bf),
        dma((6,)), dma((4, 3)), dma((4, 3)), dma((3,)), dma((3,)), dma((8,)), dma((8,)),
        dma((2, n, 3)), dma((2, n, 2, 4)), dma((2, n, NZ)), dma((2, n, steps, 3)), dma((2, n, steps, 3)),
        dma((2, n, steps)), dma((2, n, 2, 4)), dma((2, n, 3)),
    ]
    hbm = pl.BlockSpec(memory_space=pl.ANY)
    smem = pl.BlockSpec(memory_space=pltpu.SMEM)
    vmem = pl.BlockSpec(memory_space=pltpu.VMEM)
    out = pl.pallas_call(
        body,
        out_shape=jax.ShapeDtypeStruct((2, HALF, WID), bf),
        in_specs=[hbm, hbm, hbm, smem, smem, vmem, hbm, hbm, hbm],
        out_specs=vmem,
        scratch_shapes=scratch,
        compiler_params=pltpu.CompilerParams(
            collective_id=0, has_side_effects=True, vmem_limit_bytes=60 * 2**20
        ),
        cost_estimate=pl.CostEstimate(flops=10**10, bytes_accessed=3 * 10**6, transcendentals=10**6),
        name="block",
    )(queries, keys, values, window, counts, gain.reshape(1, WID), w_gate, w_up, w_down)
    return out.reshape(TOK, WID)


def solution(mesh):
    in_specs = (
        P("tm", "mp"),
        P("tm", "mp"),
        P("tm", "mp"),
        P("tm"),
        P("tm"),
        P("mp"),
        P("mp", "tm"),
        P("mp", "tm"),
        P("tm", "mp"),
    )
    return jax.shard_map(
        per_device, mesh=mesh, in_specs=in_specs, out_specs=P("tm", "mp"), check_vma=False
    )
```

time: 525 us -> 209 us (0.40)
  waiting for transfers between devices: 403 us -> 0 us
  Pallas kernels: 0 us -> 201 us
  starting transfers between devices: 37.5 us -> 0 us
  matrix products: 24.7 us -> 0 us
  blocking collectives: 23.1 us -> 0 us
  between operations: 14.7 us -> 1.31 us
  other arithmetic: 7.66 us -> 0 us
  local copies, waits for them, and re-layouts: 10.5 us -> 2.88 us
    reduce_scatter x2 -> x0, waiting for transfers between devices: 239 us -> none  [the longest x1 120 us: per_device(): lax.psum_scatter(jnp.dot(hidden, w_down, preferred_element_type=jnp.float...]
    pallas_call x0 -> x1, Pallas kernels: none -> 201 us  [per_device(): pl.pallas_call(body, out_shape=jax.ShapeDtypeStruct((2, HALF, WID), bf),...]
    all_gather x2 -> x0, waiting for transfers between devices: 148 us -> none  [the longest x1 74.8 us: per_device(): hidden = lax.all_gather(hidden_share, 'mp', axis=0, tiled=True)]
    ppermute x12 -> x0, starting transfers between devices: 37.4 us -> none  [shifted(): lax.ppermute(value, axis, [(source, source + steps) for source in range(i...]
    psum x1 -> x0, blocking collectives: 23.1 us -> none  [per_device(): squares = lax.psum(jnp.sum(attended * attended, axis=1), 'mp')]
    dot_general x3 -> x0, matrix products: 21.3 us -> none  [the longest x1 10.9 us: per_device(): jnp.dot(lax.all_gather(normed, 'tm', axis=0, tiled=True), both, preferred...]
    ppermute x12 -> x0, waiting for transfers between devices: 15.8 us -> none  [shifted(): lax.ppermute(value, axis, [(source, source + steps) for source in range(i...]
    unnamed x20 -> x1, local copies, waits for them, and re-layouts: 8.75 us -> 1.62 us
  transfers between devices with their start and end apart: 16 -> 0, of which waited for: 9 -> 0; matrix products, arithmetic and copies ran while one was open for 2% -> 0% of each run, Pallas kernels for 0% -> 0%
where the time goes in v1:
time: 209 us; the launch traced here: 205 us
  Pallas kernels  201 us (96%)
  local copies, waits for them, and re-layouts  2.88 us (1%)
    pallas_call x1, Pallas kernels, per_device(): pl.pallas_call(body, out_shape=jax.ShapeDtypeStruct((2, HALF, WID), bf),...  201 us

profile of v1, /device:TPU:1, one launch (start us, length us, event | category | flops | bytes accessed | tf_op | source)
XLA Modules:
  0.0 205.4 jit_solution(3236261133934039289)
XLA Ops:
  1.3 1.3 reshape.6.gain_ref
  2.6 201.3 %block.1 = bf16[2,64,768]{2,1,0:T(8,128)(2,1)} custom-call(bf16[128,768]{1,0:T(8,128)(2,1)} %q_hbm.1, bf16[128,768]{1,0:T(8,128)(2,1)} %k_hbm.1, bf16[128,768]{1,0:T(8,128)(2,1)} %v_hbm.1, s32[1]{0:T(128)S(6)} %copy.11.win_ref, s32[1]{0:T(128)S(6)} %copy.12.cnt_ref, f32[1,768]{1,0:T(1,128)} %reshape.6.gain_ref, bf16[768,512]{1,0:T(8,128)(2,1)} %wg_hbm.1, ...), custom_call_target="tpu_custom_call" | custom-call | flops 10000000000 | bytes 3000000 | tf_op jit(solution)/shard_map/block/pallas_call | solution.py:379
  203.8 1.6 copy.13

commit v2 on v1

--- a/solution.py
+++ b/solution.py
@@ -15,20 +15,26 @@
 HALF = 64
 WID = 768
 HID = 512
+QUART = 256
 NX = 4
 NZ = 8
-SPLITS = ((0, 32), (32, 32))
+SPLITS = ((0, 16), (16, 16), (32, 16), (48, 16))
 SLOT = {0: 0, 1: 1, -1: 2, 2: 3, -2: 4, 3: 5, -3: 6, 4: 7}
 GROUPS = ((0, 1), (1, 2), (3, 2), (5, 2), (7, 1))
+STEPS = tuple((i, m) for m in range(5) for i in (0, 1)) + tuple((i, 4 - m) for m in range(5) for i in (2, 3))
+LAGS = (0, 1, 2, 3, 5, 6)
+GATHERS = ((None, 1, 3, 4, 7), (0, 2, 3, 5, 8), (1, 3, 6, 8, 9), (1, 4, 7, 8, 10))
+EARLY = 2
+HOLD = ((0, 3, 3, 1, 0, 2), (0, 3, 2, 2, 2, 1), (1, 1, 0, 0, 1, 2), (0, 0, 0, 0, 2, 2))
 
 
 def body(
     q_hbm, k_hbm, v_hbm, win_ref, cnt_ref, gain_ref, wg_hbm, wu_hbm, wd_hbm, out_ref, *scratch
 ):
     (q_ref, k_ref, v_ref, cn_ref, s_ref, att_ref, ss_ref, nrm_ref, wgu_ref, wd_ref) = scratch[:10]
-    (x_refs, ps_refs, pr_refs, h_refs, os_refs, oc_refs, oo_refs, rs_refs, rr_refs, f_refs) = scratch[10:20]
-    (load_sem, kv_send, kv_recv, w_send, w_recv, ss_send, ss_recv) = scratch[20:27]
-    (y_sem, ag_sem, rl_sem, p_sem, h_sem, o_sem, r_sem, f_sem) = scratch[27:35]
+    (x_refs, ps_refs, pa_refs, pr_refs, h_refs, os_refs, oc_refs, oo_refs, rs_refs, rr_refs, f_refs) = scratch[10:21]
+    (load_sem, kv_send, kv_recv, w_send, w_recv, ss_send, ss_recv) = scratch[21:28]
+    (y_sem, ag_sem, rl_sem, pa_sem, p_sem, h_sem, hf_sem, o_sem, r_sem, f_sem) = scratch[28:38]
 
     tm = lax.axis_index("tm")
     mp = lax.axis_index("mp")
@@ -40,11 +46,15 @@
 
     z_up, z_down = lax.rem(z + 1, NZ), lax.rem(z + NZ - 1, NZ)
     core = dev(c_=1 - c)
-    y_l, y_h, y_lh = dev(yl_=1 - yl), dev(yh_=1 - yh), dev(yl_=1 - yl, yh_=1 - yh)
+    y_l, y_h = dev(yl_=1 - yl), dev(yh_=1 - yh)
     ups = (dev(z_=z_up), dev(z_=z_down))
     xs = [lax.rem(x + j, NX) for j in range(NX)]
     x_dev = [dev(x_=xs[j]) for j in range(NX)]
     xh_dev = [dev(x_=xs[j], yh_=1 - yh) for j in range(NX)]
+    mate, mate_l = dev(x_=x + 1 - 2 * (x % 2)), dev(x_=x + 1 - 2 * (x % 2), yl_=1 - yl)
+    th = ((x + 1) // 2) % 2
+    xa = x // 2
+    across = (dev(x_=3 - x), y_h)
     next_chip = (lax.rem(tm + 2, 32), mp)
     prev_chip = (lax.rem(tm + 30, 32), mp)
 
@@ -62,8 +72,9 @@
     loads = []
     for i, (src, dst) in enumerate((
         (k_hbm, k_ref.at[0]), (v_hbm, v_ref.at[0]), (q_hbm, q_ref),
-        (wg_hbm, wgu_ref.at[0, :, pl.ds(0, HID)]), (wu_hbm, wgu_ref.at[0, :, pl.ds(HID, HID)]),
         (wd_hbm, wd_ref.at[0]),
+        *((w.at[:, pl.ds(half * QUART, QUART)], wgu_ref.at[0, :, pl.ds((2 * half + j) * QUART, QUART)])
+          for half in range(2) for j, w in enumerate((wg_hbm, wu_hbm))),
     )):
         copy = pltpu.make_async_copy(src, dst, load_sem.at[i])
         copy.start()
@@ -72,7 +83,7 @@
     cn_ref[0] = jnp.full((8, 128), cnt_ref[0], jnp.int32)
 
     barrier = pltpu.get_barrier_semaphore()
-    partners = (core, y_l, y_h, y_lh, *ups, *x_dev[1:], *xh_dev[1:], next_chip, prev_chip)
+    partners = (core, y_l, y_h, mate_l, *ups, *x_dev[1:], *xh_dev[1:], next_chip, prev_chip)
     for device in partners:
         pl.semaphore_signal(barrier, inc=1, device_id=device, device_id_type=MESH)
     pl.semaphore_wait(barrier, len(partners))
@@ -86,9 +97,11 @@
     loads[1].wait()
     own = [kv_copy(i, 0, 2, 0, next_chip) for i in range(3)]
     w_copies = [
-        remote(wg_hbm, wgu_ref.at[1, :, pl.ds(0, HID)], w_send.at[0], w_recv.at[0], y_h),
-        remote(wu_hbm, wgu_ref.at[1, :, pl.ds(HID, HID)], w_send.at[1], w_recv.at[1], y_h),
-        remote(wd_hbm, wd_ref.at[1], w_send.at[2], w_recv.at[2], y_h),
+        remote(
+            w.at[:, pl.ds(half * QUART, QUART)], wgu_ref.at[1, :, pl.ds((2 * half + j) * QUART, QUART)],
+            w_send.at[2 * half + j], w_recv.at[2 * half + j], mate,
+        )
+        for half in range(2) for j, w in enumerate((wg_hbm, wu_hbm))
     ]
     loads[2].wait()
 
@@ -155,13 +168,15 @@
         nrm_ref[:, :, cols] = normed.reshape(2, HALF, HD)
 
     y_copies = []
-    for i, (off, size) in enumerate(SPLITS):
+
+    def spread(i):
+        off, size = SPLITS[i]
         rows = pl.ds(off, size)
-        x_refs[i][0, 0, 0, 0] = nrm_ref[yh, rows]
+        x_refs[i][0, 0, 0, 0] = nrm_ref[th, rows]
         y_copies.append([
-            remote(nrm_ref.at[1 - yh, rows], x_refs[i].at[0, 0, 1, 0], y_sem.at[0, i, 0], y_sem.at[1, i, 0], y_h),
-            remote(nrm_ref.at[yh, rows], x_refs[i].at[0, 0, 0, 1], y_sem.at[0, i, 1], y_sem.at[1, i, 1], y_l),
-            remote(nrm_ref.at[1 - yh, rows], x_refs[i].at[0, 0, 1, 1], y_sem.at[0, i, 2], y_sem.at[1, i, 2], y_lh),
+            remote(nrm_ref.at[1 - th, rows], x_refs[i].at[0, 0, 1, 0], y_sem.at[0, i, 0], y_sem.at[1, i, 0], mate),
+            remote(nrm_ref.at[th, rows], x_refs[i].at[0, 0, 0, 1], y_sem.at[0, i, 1], y_sem.at[1, i, 1], y_l),
+            remote(nrm_ref.at[1 - th, rows], x_refs[i].at[0, 0, 1, 1], y_sem.at[0, i, 2], y_sem.at[1, i, 2], mate_l),
         ])
 
     ring, relay = {}, {}
@@ -198,7 +213,7 @@
         if m == 4:
             relay_send(i, SLOT[4])
 
-    p_copies, h_copies, o_copies, r_copies, f_copies = {}, {}, {}, {}, {}
+    pa_copies, p_copies, h_copies, hf_copies, o_copies, r_copies, f_copies = {}, {}, {}, {}, {}, {}, {}
 
     def gate_up(i, m):
         slot, count = GROUPS[m]
@@ -211,36 +226,75 @@
                 tokens = x_refs[i][slot : slot + count, :, half].reshape(count * 4 * size, WID)
                 part = jnp.dot(tokens, wgu_ref[half, :, n : n + 256], preferred_element_type=jnp.float32)
                 acc = part if acc is None else acc + part
-            ps_refs[i][slot : slot + count, :, :, n : n + 256] = acc.astype(jnp.bfloat16).reshape(
-                count, 4, size, 256
+            ps_refs[i][slot : slot + count, :, :, :, n : n + 256] = acc.astype(jnp.bfloat16).reshape(
+                count, 2, 2, size, 256
             )
-        p_copies[i, m] = [
+        slots = pl.ds(slot, count)
+        out = (
+            ps_refs[i].at[slots, 1 - xa, :, :, pl.ds(0, HID)],
+            ps_refs[i].at[slots, :, 1 - yh, :, pl.ds(HID, HID)],
+        )
+        pa_copies[i, m] = [
             remote(
-                ps_refs[i].at[pl.ds(slot, count), xs[j]], pr_refs[i].at[pl.ds(slot, count), j - 1],
-                p_sem.at[0, i, m, j - 1], p_sem.at[1, i, m, j - 1], x_dev[j],
+                out[way], pa_refs[i].at[slots, way], pa_sem.at[0, i, m, way], pa_sem.at[1, i, m, way], across[way]
             )
-            for j in (2, 1, 3)
+            for way in range(2)
         ]
 
+    def combine(i, m):
+        slot, count = GROUPS[m]
+        slots = pl.ds(slot, count)
+        p_copies[i, m] = []
+        for way in range(2):
+            pa_copies[i, m][way].wait_recv()
+            cols = pl.ds(way * HID, HID)
+            a, b = ((xa, 1 - yh), (1 - xa, yh))[way]
+            for k in range(slot, slot + count):
+                ps_refs[i][k, a, b, :, cols] = (
+                    ps_refs[i][k, a, b, :, cols].astype(jnp.float32)
+                    + pa_refs[i][k, way, (b, a)[way]].astype(jnp.float32)
+                ).astype(jnp.bfloat16)
+            p_copies[i, m].append(remote(
+                ps_refs[i].at[slots, a, b, :, cols], pr_refs[i].at[slots, way],
+                p_sem.at[0, i, m, way], p_sem.at[1, i, m, way], across[1 - way],
+            ))
+
     def hidden(i, m):
         slot, count = GROUPS[m]
-        for copy in p_copies[i, m]:
-            copy.wait_recv()
-        for k in range(slot, slot + count):
-            both = ps_refs[i][k, x].astype(jnp.float32)
-            for j in range(NX - 1):
-                both = both + pr_refs[i][k, j].astype(jnp.float32)
-            gate, up = both[:, :HID], both[:, HID:]
-            h_refs[i][k, x] = (gate / (1.0 + jnp.exp(-gate)) * up).astype(jnp.bfloat16)
-        ref = h_refs[i].at[pl.ds(slot, count), x]
-        h_copies[i, m] = [
-            remote(ref, ref, h_sem.at[0, i, m, j - 1], h_sem.at[1, i, m, j - 1], x_dev[j]) for j in (2, 1, 3)
-        ]
+        slots = pl.ds(slot, count)
+        h_copies[i, m] = []
+        for way in range(2):
+            p_copies[i, m][way].wait_recv()
+            cols = pl.ds(way * QUART, QUART)
+            for k in range(slot, slot + count):
+                both = (
+                    ps_refs[i][k, xa, yh, :, pl.ds(way * HID, HID)].astype(jnp.float32)
+                    + pa_refs[i][k, way, (yh, xa)[way]].astype(jnp.float32)
+                    + pr_refs[i][k, way].astype(jnp.float32)
+                )
+                gate, up = both[:, :QUART], both[:, QUART:]
+                h_refs[i][k, xa, yh, :, cols] = (gate / (1.0 + jnp.exp(-gate)) * up).astype(jnp.bfloat16)
+            ref = h_refs[i].at[slots, xa, yh, :, cols]
+            h_copies[i, m].append(
+                remote(ref, ref, h_sem.at[0, i, m, way], h_sem.at[1, i, m, way], across[1 - way])
+            )
+
+    def forward(i, m):
+        slot, count = GROUPS[m]
+        slots = pl.ds(slot, count)
+        hf_copies[i, m] = []
+        for way in range(2):
+            h_copies[i, m][way].wait_recv()
+            cols = pl.ds(way * QUART, QUART)
+            ref = (h_refs[i].at[slots, xa, :, :, cols], h_refs[i].at[slots, :, yh, :, cols])[way]
+            hf_copies[i, m].append(
+                remote(ref, ref, hf_sem.at[0, i, m, way], hf_sem.at[1, i, m, way], across[way])
+            )
 
     def down(i, m):
         slot, count = GROUPS[m]
         size = SPLITS[i][1]
-        for copy in h_copies[i, m]:
+        for copy in hf_copies[i, m]:
             copy.wait_recv()
         rows = h_refs[i][slot : slot + count].reshape(count * 4 * size, HID)
         for half in range(2):
@@ -287,7 +341,7 @@
         ref = oo_refs[i]
         own = rr_refs[i]
         ref[0] += own[0, 3].astype(jnp.float32) + own[1, 3].astype(jnp.float32)
-        for j, (half, group, device) in enumerate(((0, 1, y_l), (1, 0, y_h), (1, 1, y_lh))):
+        for j, (half, group, device) in enumerate(((0, 1, y_l), (1, 0, mate), (1, 1, mate_l))):
             f_refs[i][0, j] = ref[0, half, group].astype(jnp.bfloat16)
             f_copies[i, j] = remote(
                 f_refs[i].at[0, j], f_refs[i].at[1, j], f_sem.at[0, i, j], f_sem.at[1, i, j], device
@@ -301,37 +355,49 @@
         got = f_refs[i]
         mine = oo_refs[i][0, 0, 0] + got[1, 0].astype(jnp.float32)
         theirs = got[1, 1].astype(jnp.float32) + got[1, 2].astype(jnp.float32)
-        out_ref[yh, rows] = (nrm_ref[yh, rows].astype(jnp.float32) + mine).astype(jnp.bfloat16)
-        out_ref[1 - yh, rows] = (nrm_ref[1 - yh, rows].astype(jnp.float32) + theirs).astype(jnp.bfloat16)
-
-    steps = [(i, m) for i in range(len(SPLITS)) for m in range(len(GROUPS))]
-    for i in range(len(SPLITS)):
-        gather(i, 0)
+        out_ref[th, rows] = (nrm_ref[th, rows].astype(jnp.float32) + mine).astype(jnp.bfloat16)
+        out_ref[1 - th, rows] = (nrm_ref[1 - th, rows].astype(jnp.float32) + theirs).astype(jnp.bfloat16)
+
+    stages = (gate_up, combine, hidden, forward, down, both_cores)
+    last = LAGS[-1]
+    gathers = sorted(
+        (at, i, m) for i, row in enumerate(GATHERS) for m, at in enumerate(row) if at is not None
+    )
+    tails = []
+    for i, hold in enumerate(HOLD):
+        at = 0
+        for j in range(6):
+            ready = last + STEPS.index((i, max(4 - j, 0)))
+            at = max(at + 1 + (hold[j] if j > 3 else 0), ready + (hold[j] if j < 5 else 0))
+            part = functools.partial(sums, i, j) if j < 4 else functools.partial((deliver, finish)[j - 4], i)
+            tails.append((at, part))
+    tails.sort(key=lambda t: t[0])
+
+    def run_gathers(k):
+        while gathers and gathers[0][0] <= k:
+            gather(*gathers.pop(0)[1:])
+
+    spread(0)
+    gather(0, 0)
+    for i in range(1, len(SPLITS)):
+        spread(i)
+    run_gathers(EARLY - 1)
     for copy in loads[3:]:
         copy.wait()
-    for copy in w_copies[:2]:
+    for copy in w_copies:
         copy.wait_recv()
-    tail = []
-    for k in range(len(steps) + 3):
-        if k < len(steps):
-            gate_up(*steps[k])
-        if k + 1 < len(steps) and steps[k + 1][1] > 0:
-            gather(*steps[k + 1])
-        if 0 <= k - 1 < len(steps):
-            hidden(*steps[k - 1])
-        if 0 <= k - 2 < len(steps):
-            if k == 2:
-                w_copies[2].wait_recv()
-            down(*steps[k - 2])
-        if 0 <= k - 3 < len(steps):
-            i, m = steps[k - 3]
-            both_cores(i, m)
-            if m == len(GROUPS) - 1:
-                tail += [functools.partial(sums, i, r) for r in range(4)]
-                tail += [functools.partial(deliver, i), functools.partial(finish, i)]
-        if tail:
-            tail.pop(0)()
-    for part in tail:
+    w_copies.append(remote(wd_hbm, wd_ref.at[1], w_send.at[4], w_recv.at[4], mate))
+    for k in range(len(STEPS) + last):
+        for lag, stage in zip(LAGS, stages):
+            if 0 <= k - lag < len(STEPS):
+                if stage is down and k == lag:
+                    w_copies[4].wait_recv()
+                stage(*STEPS[k - lag])
+            if lag == 0:
+                run_gathers(k)
+        while tails and tails[0][0] <= k:
+            tails.pop(0)[1]()
+    for _, part in tails:
         part()
 
     for copy in sent:
@@ -360,17 +426,19 @@
         pltpu.VMEM((2, WID, 2 * HID), bf),
         pltpu.VMEM((2, HID, WID), bf),
         each(lambda s: (NZ, 2, 2, 2, s, WID), bf),
-        each(lambda s: (NZ, NX, s, 2 * HID), bf),
-        each(lambda s: (NZ, NX - 1, s, 2 * HID), bf),
-        each(lambda s: (NZ, NX, s, HID), bf),
+        each(lambda s: (NZ, 2, 2, s, 2 * HID), bf),
+        each(lambda s: (NZ, 2, 2, s, HID), bf),
+        each(lambda s: (NZ, 2, s, HID), bf),
+        each(lambda s: (NZ, 2, 2, s, HID), bf),
         each(lambda s: (NZ, 2, 2, s, WID), bf),
         each(lambda s: (NZ, 2, 2, s, WID), bf),
         each(lambda s: (NZ, 2, 2, s, WID), f32),
         each(lambda s: (2, 4, 2, 2, s, WID), bf),
         each(lambda s: (2, 4, 2, 2, s, WID), bf),
         each(lambda s: (2, 3, s, WID), bf),
-        dma((6,)), dma((4, 3)), dma((4, 3)), dma((3,)), dma((3,)), dma((8,)), dma((8,)),
-        dma((2, n, 3)), dma((2, n, 2, 4)), dma((2, n, NZ)), dma((2, n, steps, 3)), dma((2, n, steps, 3)),
+        dma((8,)), dma((4, 3)), dma((4, 3)), dma((5,)), dma((5,)), dma((8,)), dma((8,)),
+        dma((2, n, 3)), dma((2, n, 2, 4)), dma((2, n, NZ)), dma((2, n, steps, 2)), dma((2, n, steps, 2)),
+        dma((2, n, steps, 2)), dma((2, n, steps, 2)),
         dma((2, n, steps)), dma((2, n, 2, 4)), dma((2, n, 3)),
     ]
     hbm = pl.BlockSpec(memory_space=pl.ANY)

time: 209 us -> 155 us (0.74); the launches traced: 205 us -> 155 us
  Pallas kernels: 201 us -> 151 us
    pallas_call x1, Pallas kernels: 201 us -> 151 us  [per_device(): pl.pallas_call(body, out_shape=jax.ShapeDtypeStruct((2, HALF, WID), bf),...]
where the time goes in v2:
time: 155 us
  Pallas kernels  151 us (97%)
  local copies, waits for them, and re-layouts  2.88 us (2%)
    pallas_call x1, Pallas kernels, per_device(): pl.pallas_call(body, out_shape=jax.ShapeDtypeStruct((2, HALF, WID), bf),...  151 us

profile of v2, /device:TPU:1, one launch (start us, length us, event | category | flops | bytes accessed | tf_op | source)
XLA Modules:
  0.0 155.0 jit_solution(8356327674644727964)
XLA Ops:
  1.3 1.3 reshape.6.gain_ref
  2.6 150.8 %block.1 = bf16[2,64,768]{2,1,0:T(8,128)(2,1)} custom-call(bf16[128,768]{1,0:T(8,128)(2,1)} %q_hbm.1, bf16[128,768]{1,0:T(8,128)(2,1)} %k_hbm.1, bf16[128,768]{1,0:T(8,128)(2,1)} %v_hbm.1, s32[1]{0:T(128)S(6)} %copy.11.win_ref, s32[1]{0:T(128)S(6)} %copy.12.cnt_ref, f32[1,768]{1,0:T(1,128)} %reshape.6.gain_ref, bf16[768,512]{1,0:T(8,128)(2,1)} %wg_hbm.1, ...), custom_call_target="tpu_custom_call" | custom-call | flops 10000000000 | bytes 3000000 | tf_op jit(solution)/shard_map/block/pallas_call | solution.py:447
  153.4 1.6 %copy.13 = bf16[128,768]{1,0:T(8,128)(2,1)} copy(bf16[128,768]{1,0:T(8,128)(2,1)} %bitcast.1) | data formatting | bytes 393216

commit v3 on v2

v3 whole, which is shorter than its diff:
```python
import functools

import jax
import jax.numpy as jnp
from jax import lax
from jax.experimental import pallas as pl
from jax.experimental.pallas import tpu as pltpu
from jax.sharding import PartitionSpec as P

MESH = pl.DeviceIdType.MESH
HD = 128
D = 6144
WMAX = 4
TOK = 128
HALF = 64
WID = 768
HID = 512
QUART = 256
NX = 4
NZ = 8
SPLITS = ((0, 16), (16, 16), (32, 16), (48, 16))
NEAR = {0: 0, 1: 1, -1: 2, 2: 3, -2: 4, 3: 5, -3: 6, 4: 7}
FAR = {-1: 0, 0: 1, -2: 2, 1: 3, -3: 4, 2: 5, 4: 6, 3: 7}
SLOTS = (NEAR, NEAR, FAR, FAR)
GROUPS = ((0, 1), (1, 2), (3, 2), (5, 2), (7, 1))
STEPS = tuple((i, m) for m in range(5) for i in (0, 1)) + tuple((i, 4 - m) for m in range(5) for i in (2, 3))
LAGS = (0, 1, 2, 3, 4, 5)
GATHERS = ((None, 1, 3, 5, 6), (-13, 2, 4, 6, 7), (-10, 5, 6, 8, 10), (3, 5, 7, 9, 10))
EARLY = 0
SECOND, DOWN = 6, 10
HOLD = ((2, 2, 2, 1, 5, 4), (0, 2, 2, 2, 4, 2), (0, 1, 1, 0, 1, 7), (0, 1, 0, 0, 4, 5))


def body(
    q_hbm, k_hbm, v_hbm, win_ref, cnt_ref, gain_ref, wg_hbm, wu_hbm, wd_hbm, out_ref, *scratch
):
    (qo_ref, q_ref, k_ref, v_ref, cn_ref, s_ref, att_ref, ss_ref, nrm_ref, wgu_ref, wd_ref) = scratch[:11]
    (x_refs, ps_refs, pa_refs, pr_refs, h_refs, os_refs, oc_refs, oo_refs, rs_refs, rr_refs, f_refs) = scratch[11:22]
    (load_sem, kv_send, kv_recv, w_send, w_recv, ss_send, ss_recv) = scratch[22:29]
    (y_sem, ag_sem, rl_sem, pa_sem, p_sem, h_sem, hf_sem, o_sem, r_sem, f_sem) = scratch[29:39]

    tm = lax.axis_index("tm")
    mp = lax.axis_index("mp")
    yl, z, c = tm // 16, (tm // 2) % NZ, tm % 2
    x, yh = mp // 2, mp % 2

    def dev(yl_=yl, z_=z, c_=c, x_=x, yh_=yh):
        return (yl_ * 16 + z_ * 2 + c_, x_ * 2 + yh_)

    z_up, z_down = lax.rem(z + 1, NZ), lax.rem(z + NZ - 1, NZ)
    core = dev(c_=1 - c)
    y_l, y_h = dev(yl_=1 - yl), dev(yh_=1 - yh)
    ups = (dev(z_=z_up), dev(z_=z_down))
    xs = [lax.rem(x + j, NX) for j in range(NX)]
    x_dev = [dev(x_=xs[j]) for j in range(NX)]
    xh_dev = [dev(x_=xs[j], yh_=1 - yh) for j in range(NX)]
    mate, mate_l = dev(x_=x + 1 - 2 * (x % 2)), dev(x_=x + 1 - 2 * (x % 2), yl_=1 - yl)
    th = ((x + 1) // 2) % 2
    xa = x // 2
    across = (dev(x_=3 - x), y_h)
    next_chip = (lax.rem(tm + 2, 32), mp)
    prev_chip = (lax.rem(tm + 30, 32), mp)

    sent = []

    def remote(src, dst, send_sem, recv_sem, device):
        copy = pltpu.make_async_remote_copy(
            src_ref=src, dst_ref=dst, send_sem=send_sem, recv_sem=recv_sem,
            device_id=device, device_id_type=MESH,
        )
        copy.start()
        sent.append(copy)
        return copy

    loads = []
    for i, (src, dst) in enumerate((
        (q_hbm, qo_ref), (k_hbm, k_ref.at[2]), (v_hbm, v_ref.at[2]),
        (wd_hbm, wd_ref.at[0]),
        *((w.at[:, pl.ds(half * QUART, QUART)], wgu_ref.at[0, :, pl.ds((2 * half + j) * QUART, QUART)])
          for half in range(2) for j, w in enumerate((wg_hbm, wu_hbm))),
    )):
        copy = pltpu.make_async_copy(src, dst, load_sem.at[i])
        copy.start()
        loads.append(copy)

    first = lax.broadcasted_iota(jnp.int32, (8, 128), 0) == 0
    cn_ref[2] = jnp.where(
        first, jnp.full((8, 128), cnt_ref[0], jnp.int32), jnp.full((8, 128), win_ref[0], jnp.int32)
    )

    barrier = pltpu.get_barrier_semaphore()
    partners = (core, y_l, y_h, mate_l, *ups, *x_dev[1:], *xh_dev[1:], next_chip, prev_chip)
    for device in partners:
        pl.semaphore_signal(barrier, inc=1, device_id=device, device_id_type=MESH)
    pl.semaphore_wait(barrier, len(partners))

    kv = (cn_ref, k_ref, v_ref)

    def kv_copy(i, src, dst, sem, device):
        return remote(kv[i].at[src], kv[i].at[dst], kv_send.at[sem, i], kv_recv.at[sem, i], device)

    w_copies = []

    def send_weights(half):
        for j, w in enumerate((wg_hbm, wu_hbm)):
            w_copies.append(remote(
                w.at[:, pl.ds(half * QUART, QUART)], wgu_ref.at[1, :, pl.ds((2 * half + j) * QUART, QUART)],
                w_send.at[2 * half + j], w_recv.at[2 * half + j], mate,
            ))

    below = [kv_copy(0, 2, 0, 0, prev_chip)]
    above = [kv_copy(0, 2, 4, 1, next_chip)]
    loads[0].wait()
    q_copy = remote(qo_ref, q_ref, kv_send.at[4, 0], kv_recv.at[4, 0], prev_chip)
    for i in (1, 2):
        loads[i].wait()
        below.append(kv_copy(i, 2, 0, 0, prev_chip))
        above.append(kv_copy(i, 2, 4, 1, next_chip))
    send_weights(0)

    keys_at = lax.broadcasted_iota(jnp.int32, (1, TOK), 1)
    place = jnp.full((1, TOK), lax.rem(tm + 2, 32), jnp.int32)

    def score(e):
        visible = keys_at < cn_ref[e, 0:1, :]
        if e > 0:
            visible = visible & (cn_ref[0, 1:2, :] >= e) & (place >= e)
        for h in range(WID // HD):
            cols = pl.ds(h * HD, HD)
            s = lax.dot_general(
                q_ref[:, cols], k_ref[e, :, cols], (((1,), (1,)), ((), ())),
                preferred_element_type=jnp.float32,
            ) * HD ** (-0.5)
            s_ref[h, :, pl.ds(e * TOK, TOK)] = jnp.where(visible, s, -1e30)

    q_copy.wait_recv()
    below[0].wait_recv()
    score(2)
    near, mid = [], []
    for i in range(3):
        above[i].wait_recv()
        mid.append(kv_copy(i, 2 * c + 2, 3, 3, core))
    score(4)
    for i in range(3):
        if i > 0:
            below[i].wait_recv()
        near.append(kv_copy(i, 2 * c, 1, 2, core))
    score(0)
    for i in range(3):
        mid[i].wait_recv()
    score(3)
    for i in range(3):
        near[i].wait_recv()
    score(1)

    squares = jnp.zeros((TOK, HD), jnp.float32)
    for h in range(WID // HD):
        cols = pl.ds(h * HD, HD)
        s = s_ref[h]
        expo = jnp.exp(s - jnp.max(s, axis=-1, keepdims=True))
        total = jnp.sum(expo, axis=-1, keepdims=True)
        vals = v_ref[:, :, cols].reshape((WMAX + 1) * TOK, HD)
        att = jnp.dot(expo.astype(jnp.bfloat16), vals, preferred_element_type=jnp.float32) / total
        att_ref[:, cols] = att
        squares = squares + att * att
    row = jnp.broadcast_to(jnp.sum(squares, axis=1, keepdims=True), (TOK, TOK))
    ss_ref[0] = jnp.transpose(row)[0:8]
    ss_copies = [
        remote(ss_ref.at[0], ss_ref.at[j], ss_send.at[j], ss_recv.at[j], device)
        for j, device in enumerate((y_h, *x_dev[1:], *xh_dev[1:]), start=1)
    ]
    for copy in ss_copies:
        copy.wait_recv()
    total = ss_ref[0]
    for j in range(1, 8):
        total = total + ss_ref[j]
    factor = lax.rsqrt(total / D + 1e-06)
    factor = jnp.transpose(jnp.broadcast_to(factor[0:1], (TOK, TOK)))
    for h in range(WID // HD):
        cols = pl.ds(h * HD, HD)
        normed = (att_ref[:, cols] * factor * gain_ref[cols].reshape(1, HD)).astype(jnp.bfloat16)
        nrm_ref[:, :, cols] = normed.reshape(2, HALF, HD)

    y_copies = []

    def spread(i):
        off, size = SPLITS[i]
        rows = pl.ds(off, size)
        x_refs[i][SLOTS[i][0], 0, 0, 0] = nrm_ref[th, rows]
        y_copies.append([
            remote(nrm_ref.at[1 - th, rows], x_refs[i].at[SLOTS[i][0], 0, 1, 0], y_sem.at[0, i, 0], y_sem.at[1, i, 0], mate),
            remote(nrm_ref.at[th, rows], x_refs[i].at[SLOTS[i][0], 0, 0, 1], y_sem.at[0, i, 1], y_sem.at[1, i, 1], y_l),
            remote(nrm_ref.at[1 - th, rows], x_refs[i].at[SLOTS[i][0], 0, 1, 1], y_sem.at[0, i, 2], y_sem.at[1, i, 2], mate_l),
        ])

    ring, relay = {}, {}

    def ring_send(i, way, m):
        sign = (-1, 1)[way]
        src = SLOTS[i][sign * (m - 1)]
        dst = SLOTS[i][4 if m == 4 else sign * m]
        src_ref, dst_ref = x_refs[i].at[src, 0], x_refs[i].at[dst, 0]
        if m == 4:
            src_ref, dst_ref = src_ref.at[way], dst_ref.at[way]
        ring[i, way, m] = remote(
            src_ref, dst_ref, ag_sem.at[0, i, way, m - 1], ag_sem.at[1, i, way, m - 1], ups[way]
        )

    def relay_send(i, slot):
        relay[i, slot] = remote(
            x_refs[i].at[slot, 0], x_refs[i].at[slot, 1], rl_sem.at[0, i, slot], rl_sem.at[1, i, slot], core
        )

    def gather(i, m):
        if m == 0:
            for copy in y_copies[i]:
                copy.wait_recv()
            ring_send(i, 0, 1)
            ring_send(i, 1, 1)
            relay_send(i, SLOTS[i][0])
            return
        for way in range(2):
            ring[i, way, m].wait_recv()
            if m < 4:
                ring_send(i, way, m + 1)
                relay_send(i, SLOTS[i][(-1, 1)[way] * m])
        if m == 4:
            relay_send(i, SLOTS[i][4])

    pa_copies, p_copies, h_copies, hf_copies, o_copies, r_copies, f_copies = {}, {}, {}, {}, {}, {}, {}

    def gate_up(i, m, way):
        slot, count = GROUPS[m]
        size = SPLITS[i][1]
        if way == 0:
            for k in range(slot, slot + count):
                relay[i, k].wait_recv()
        for n in range(way * HID, (way + 1) * HID, 256):
            acc = None
            for half in range(2):
                tokens = x_refs[i][slot : slot + count, :, half].reshape(count * 4 * size, WID)
                part = jnp.dot(tokens, wgu_ref[half, :, n : n + 256], preferred_element_type=jnp.float32)
                acc = part if acc is None else acc + part
            ps_refs[i][slot : slot + count, :, :, :, n : n + 256] = acc.astype(jnp.bfloat16).reshape(
                count, 2, 2, size, 256
            )
        slots = pl.ds(slot, count)
        out = (
            ps_refs[i].at[slots, 1 - xa, :, :, pl.ds(0, HID)],
            ps_refs[i].at[slots, :, 1 - yh, :, pl.ds(HID, HID)],
        )[way]
        pa_copies[i, m, way] = remote(
            out, pa_refs[i].at[slots, way], pa_sem.at[0, i, m, way], pa_sem.at[1, i, m, way], across[way]
        )

    def combine(i, m, way):
        slot, count = GROUPS[m]
        slots = pl.ds(slot, count)
        pa_copies[i, m, way].wait_recv()
        cols = pl.ds(way * HID, HID)
        a, b = ((xa, 1 - yh), (1 - xa, yh))[way]
        for k in range(slot, slot + count):
            ps_refs[i][k, a, b, :, cols] = (
                ps_refs[i][k, a, b, :, cols].astype(jnp.float32)
                + pa_refs[i][k, way, (b, a)[way]].astype(jnp.float32)
            ).astype(jnp.bfloat16)
        p_copies[i, m, way] = remote(
            ps_refs[i].at[slots, a, b, :, cols], pr_refs[i].at[slots, way],
            p_sem.at[0, i, m, way], p_sem.at[1, i, m, way], across[1 - way],
        )

    def hidden(i, m, way):
        slot, count = GROUPS[m]
        slots = pl.ds(slot, count)
        p_copies[i, m, way].wait_recv()
        cols = pl.ds(way * QUART, QUART)
        for k in range(slot, slot + count):
            both = (
                ps_refs[i][k, xa, yh, :, pl.ds(way * HID, HID)].astype(jnp.float32)
                + pa_refs[i][k, way, (yh, xa)[way]].astype(jnp.float32)
                + pr_refs[i][k, way].astype(jnp.float32)
            )
            gate, up = both[:, :QUART], both[:, QUART:]
            h_refs[i][k, xa, yh, :, cols] = (gate / (1.0 + jnp.exp(-gate)) * up).astype(jnp.bfloat16)
        ref = h_refs[i].at[slots, xa, yh, :, cols]
        h_copies[i, m, way] = remote(
            ref, ref, h_sem.at[0, i, m, way], h_sem.at[1, i, m, way], across[1 - way]
        )

    def forward(i, m, way):
        slot, count = GROUPS[m]
        slots = pl.ds(slot, count)
        h_copies[i, m, way].wait_recv()
        cols = pl.ds(way * QUART, QUART)
        ref = (h_refs[i].at[slots, xa, :, :, cols], h_refs[i].at[slots, :, yh, :, cols])[way]
        hf_copies[i, m, way] = remote(
            ref, ref, hf_sem.at[0, i, m, way], hf_sem.at[1, i, m, way], across[way]
        )

    def down(i, m):
        slot, count = GROUPS[m]
        size = SPLITS[i][1]
        for way in range(2):
            hf_copies[i, m, way].wait_recv()
        rows = h_refs[i][slot : slot + count].reshape(count * 4 * size, HID)
        for half in range(2):
            for n in range(0, WID, 256):
                o = jnp.dot(rows, wd_ref[half, :, n : n + 256], preferred_element_type=jnp.float32)
                o = o.reshape(count, 2, 2, size, 256)
                oo_refs[i][slot : slot + count, half, :, :, n : n + 256] = o[:, 0]
                os_refs[i][slot : slot + count, half, :, :, n : n + 256] = o[:, 1].astype(jnp.bfloat16)
        o_copies[i, m] = remote(
            os_refs[i].at[pl.ds(slot, count)], oc_refs[i].at[pl.ds(slot, count)],
            o_sem.at[0, i, m], o_sem.at[1, i, m], core,
        )

    def both_cores(i, m):
        slot, count = GROUPS[m]
        o_copies[i, m].wait_recv()
        for k in range(slot, slot + count):
            oo_refs[i][k] += oc_refs[i][k].astype(jnp.float32)

    def origin(offset):
        return 4 if offset == -3 else offset - 1

    def sums(i, r):
        for way in range(2):
            sign = (1, -1)[way]
            if r == 0:
                rs_refs[i][way, 0, 0] = oo_refs[i][SLOTS[i][3], way].astype(jnp.bfloat16)
                src, dst = rs_refs[i].at[way, 0, 0], rr_refs[i].at[way, 0, way]
            else:
                r_copies[i, way, r - 1].wait_recv()
                slot = SLOTS[i][origin(sign * (4 - r))]
                if r == 1:
                    rs_refs[i][way, 1, way] = (
                        oo_refs[i][slot, way] + rr_refs[i][way, 0, way].astype(jnp.float32)
                    ).astype(jnp.bfloat16)
                    rs_refs[i][way, 1, 1 - way] = oo_refs[i][slot, 1 - way].astype(jnp.bfloat16)
                else:
                    rs_refs[i][way, r] = (
                        oo_refs[i][slot] + rr_refs[i][way, r - 1].astype(jnp.float32)
                    ).astype(jnp.bfloat16)
                src, dst = rs_refs[i].at[way, r], rr_refs[i].at[way, r]
            r_copies[i, way, r] = remote(src, dst, r_sem.at[0, i, way, r], r_sem.at[1, i, way, r], ups[way])

    mine_at = 1 - (z + NZ - 1) // NZ

    def deliver(i):
        for way in range(2):
            r_copies[i, way, 3].wait_recv()
        ref, got, slot = oo_refs[i], rr_refs[i], SLOTS[i][-1]
        ref[slot] += got[0, 3].astype(jnp.float32) + got[1, 3].astype(jnp.float32)
        ref[slot, :, mine_at] += x_refs[i][slot, 0, :, mine_at].astype(jnp.float32)
        for j, (half, group, device) in enumerate(((0, 1 - mine_at, y_l), (1, mine_at, mate), (1, 1 - mine_at, mate_l))):
            f_refs[i][0, j] = ref[slot, half, group].astype(jnp.bfloat16)
            f_copies[i, j] = remote(
                f_refs[i].at[0, j], f_refs[i].at[1, j], f_sem.at[0, i, j], f_sem.at[1, i, j], device
            )

    def finish(i):
        off, size = SPLITS[i]
        rows = pl.ds(off, size)
        for j in range(3):
            f_copies[i, j].wait_recv()
        got = f_refs[i]
        mine = oo_refs[i][SLOTS[i][-1], 0, mine_at] + got[1, 0].astype(jnp.float32)
        theirs = got[1, 1].astype(jnp.float32) + got[1, 2].astype(jnp.float32)
        out_ref[th, rows] = mine.astype(jnp.bfloat16)
        out_ref[1 - th, rows] = theirs.astype(jnp.bfloat16)

    plan = []

    def at(step, order, part, *args):
        plan.append((step, order, len(plan), functools.partial(part, *args)))

    def weights(half):
        for copy in w_copies[2 * half : 2 * half + 2]:
            copy.wait_recv()
        if half == 1:
            w_copies.append(remote(wd_hbm, wd_ref.at[1], w_send.at[4], w_recv.at[4], mate))

    at(SECOND, 0, weights, 1)
    at(DOWN, 9, lambda: w_copies[4].wait_recv())
    done = {}
    for k, (i, m) in enumerate(STEPS):
        for way, begin in enumerate((k, max(k, SECOND))):
            for order, (lag, stage) in enumerate(zip(LAGS, (gate_up, combine, hidden, forward))):
                at(begin + lag, (1, 6, 7, 8)[order], stage, i, m, way)
        begin = max(k, SECOND, DOWN - LAGS[4])
        at(begin + LAGS[4], 10, down, i, m)
        at(begin + LAGS[5], 11, both_cores, i, m)
        done[i, m] = begin + LAGS[5]
    for i, row in enumerate(GATHERS):
        for m, step in enumerate(row):
            if step is not None:
                at(max(step, -1) if step < EARLY else step, 5 if step >= EARLY else -1, gather, i, m)
    for i, hold in enumerate(HOLD):
        step = 0
        for j in range(6):
            part = (sums, sums, sums, sums, deliver, finish)[j]
            step = max(step + 1 + (hold[j] if j > 3 else 0), done[i, max(4 - j, 0)] + (hold[j] if j < 5 else 0))
            if i < 2:
                step = max(step, done[i, 4])
            at(step, 12, part, i, *((j,) if j < 4 else ()))

    for i in range(len(SPLITS)):
        spread(i)
    for copy in w_copies:
        copy.wait_send()
    sent[:] = [copy for copy in sent if all(copy is not old for old in w_copies)]
    send_weights(1)
    gather(0, 0)
    early = [p for p in plan if p[1] == -1]
    for p in sorted(early):
        p[3]()
    for copy in loads[3:]:
        copy.wait()
    weights(0)
    for p in sorted(p for p in plan if p[1] != -1):
        p[3]()

    for copy in sent:
        copy.wait_send()


def per_device(queries, keys, values, window, counts, gain, w_gate, w_up, w_down):
    bf, f32 = jnp.bfloat16, jnp.float32
    n = len(SPLITS)
    sizes = [size for _, size in SPLITS]

    def each(shape_of, dtype):
        return [pltpu.VMEM(shape_of(size), dtype) for size in sizes]

    dma = pltpu.SemaphoreType.DMA
    steps = len(GROUPS)
    scratch = [
        pltpu.VMEM((TOK, WID), bf),
        pltpu.VMEM((TOK, WID), bf),
        pltpu.VMEM((WMAX + 1, TOK, WID), bf),
        pltpu.VMEM((WMAX + 1, TOK, WID), bf),
        pltpu.VMEM((WMAX + 1, 8, 128), jnp.int32),
        pltpu.VMEM((WID // HD, TOK, (WMAX + 1) * TOK), f32),
        pltpu.VMEM((TOK, WID), f32),
        pltpu.VMEM((8, 8, 128), f32),
        pltpu.VMEM((2, HALF, WID), bf),
        pltpu.VMEM((2, WID, 2 * HID), bf),
        pltpu.VMEM((2, HID, WID), bf),
        each(lambda s: (NZ, 2, 2, 2, s, WID), bf),
        each(lambda s: (NZ, 2, 2, s, 2 * HID), bf),
        each(lambda s: (NZ, 2, 2, s, HID), bf),
        each(lambda s: (NZ, 2, s, HID), bf),
        each(lambda s: (NZ, 2, 2, s, HID), bf),
        each(lambda s: (NZ, 2, 2, s, WID), bf),
        each(lambda s: (NZ, 2, 2, s, WID), bf),
        each(lambda s: (NZ, 2, 2, s, WID), f32),
        each(lambda s: (2, 4, 2, 2, s, WID), bf),
        each(lambda s: (2, 4, 2, 2, s, WID), bf),
        each(lambda s: (2, 3, s, WID), bf),
        dma((8,)), dma((5, 3)), dma((5, 3)), dma((5,)), dma((5,)), dma((8,)), dma((8,)),
        dma((2, n, 3)), dma((2, n, 2, 4)), dma((2, n, NZ)), dma((2, n, steps, 2)), dma((2, n, steps, 2)),
        dma((2, n, steps, 2)), dma((2, n, steps, 2)),
        dma((2, n, steps)), dma((2, n, 2, 4)), dma((2, n, 3)),
    ]
    hbm = pl.BlockSpec(memory_space=pl.ANY)
    smem = pl.BlockSpec(memory_space=pltpu.SMEM)
    vmem = pl.BlockSpec(memory_space=pltpu.VMEM)
    out = pl.pallas_call(
        body,
        out_shape=jax.ShapeDtypeStruct((2, HALF, WID), bf),
        in_specs=[hbm, hbm, hbm, smem, smem, vmem, hbm, hbm, hbm],
        out_specs=vmem,
        scratch_shapes=scratch,
        compiler_params=pltpu.CompilerParams(
            collective_id=0, has_side_effects=True, vmem_limit_bytes=60 * 2**20
        ),
        cost_estimate=pl.CostEstimate(flops=10**10, bytes_accessed=3 * 10**6, transcendentals=10**6),
        name="block",
    )(queries, keys, values, window, counts, gain, w_gate, w_up, w_down)
    return out.reshape(TOK, WID)


def solution(mesh):
    in_specs = (
        P("tm", "mp"),
        P("tm", "mp"),
        P("tm", "mp"),
        P("tm"),
        P("tm"),
        P("mp"),
        P("mp", "tm"),
        P("mp", "tm"),
        P("tm", "mp"),
    )
    return jax.shard_map(
        per_device, mesh=mesh, in_specs=in_specs, out_specs=P("tm", "mp"), check_vma=False
    )
```

time: 155 us -> 141 us (0.910)
  Pallas kernels: 151 us -> 138 us
    pallas_call x1, Pallas kernels: 151 us -> 138 us  [per_device(): pl.pallas_call(body, out_shape=jax.ShapeDtypeStruct((2, HALF, WID), bf),...]
where the time goes in v3:
time: 141 us
  Pallas kernels  138 us (98%)
  local copies, waits for them, and re-layouts  1.62 us (1%)
    pallas_call x1, Pallas kernels, per_device(): pl.pallas_call(body, out_shape=jax.ShapeDtypeStruct((2, HALF, WID), bf),...  138 us

profile of v3, /device:TPU:1, one launch (start us, length us, event | category | flops | bytes accessed | tf_op | source)
XLA Modules:
  0.0 141.3 jit_solution(673386530042405342)
XLA Ops:
  1.3 138.4 %block.1 = bf16[2,64,768]{2,1,0:T(8,128)(2,1)} custom-call(bf16[128,768]{1,0:T(8,128)(2,1)} %q_hbm.1, bf16[128,768]{1,0:T(8,128)(2,1)} %k_hbm.1, bf16[128,768]{1,0:T(8,128)(2,1)} %v_hbm.1, s32[1]{0:T(128)S(6)} %copy.11.win_ref, s32[1]{0:T(128)S(6)} %copy.12.cnt_ref, f32[768]{0:T(1024)} %gain_ref.1, bf16[768,512]{1,0:T(8,128)(2,1)} %wg_hbm.1, ...), custom_call_target="tpu_custom_call" | custom-call | flops 10000000000 | bytes 3000000 | tf_op jit(solution)/shard_map/block/pallas_call | solution.py:468
  139.7 1.6 %copy.13 = bf16[128,768]{1,0:T(8,128)(2,1)} copy(bf16[128,768]{1,0:T(8,128)(2,1)} %bitcast.1) | data formatting | bytes 393216

commit v4 on v3

--- a/solution.py
+++ b/solution.py
@@ -34,9 +34,9 @@
 def body(
     q_hbm, k_hbm, v_hbm, win_ref, cnt_ref, gain_ref, wg_hbm, wu_hbm, wd_hbm, out_ref, *scratch
 ):
-    (qo_ref, q_ref, k_ref, v_ref, cn_ref, s_ref, att_ref, ss_ref, nrm_ref, wgu_ref, wd_ref) = scratch[:11]
-    (x_refs, ps_refs, pa_refs, pr_refs, h_refs, os_refs, oc_refs, oo_refs, rs_refs, rr_refs, f_refs) = scratch[11:22]
-    (load_sem, kv_send, kv_recv, w_send, w_recv, ss_send, ss_recv) = scratch[22:29]
+    (qo_ref, q_ref, k_ref, v_ref, cn_ref, s_ref, ss_ref, nrm_ref, wgu_ref, wd_ref) = scratch[:10]
+    (x_refs, ps_refs, pa_refs, pr_refs, h_refs, os_refs, oc_refs, oo_refs, rs_refs, rr_refs, f_refs) = scratch[10:21]
+    (load_sem, kv_send, kv_recv, w_send, w_recv, ss_sem, out_sem, fac_ref) = scratch[21:29]
     (y_sem, ag_sem, rl_sem, pa_sem, p_sem, h_sem, hf_sem, o_sem, r_sem, f_sem) = scratch[29:39]
 
     tm = lax.axis_index("tm")
@@ -58,19 +58,24 @@
     th = ((x + 1) // 2) % 2
     xa = x // 2
     across = (dev(x_=3 - x), y_h)
+    yl_dev = [dev(yl_=1 - yl, x_=xs[j], yh_=b) for b in (yh, 1 - yh) for j in range(NX)]
     next_chip = (lax.rem(tm + 2, 32), mp)
     prev_chip = (lax.rem(tm + 30, 32), mp)
 
     sent = []
 
-    def remote(src, dst, send_sem, recv_sem, device):
+    def remote(src, dst, send_sem, recv_sem, device, keep=False):
         copy = pltpu.make_async_remote_copy(
             src_ref=src, dst_ref=dst, send_sem=send_sem, recv_sem=recv_sem,
             device_id=device, device_id_type=MESH,
         )
         copy.start()
-        sent.append(copy)
+        if keep:
+            sent.append(copy)
         return copy
+
+    def landed(ref, sem):
+        pltpu.make_async_copy(ref, ref, sem).wait()
 
     loads = []
     for i, (src, dst) in enumerate((
@@ -89,7 +94,7 @@
     )
 
     barrier = pltpu.get_barrier_semaphore()
-    partners = (core, y_l, y_h, mate_l, *ups, *x_dev[1:], *xh_dev[1:], next_chip, prev_chip)
+    partners = (core, y_h, *ups, *x_dev[1:], *xh_dev[1:], next_chip, prev_chip, *yl_dev)
     for device in partners:
         pl.semaphore_signal(barrier, inc=1, device_id=device, device_id_type=MESH)
     pl.semaphore_wait(barrier, len(partners))
@@ -97,7 +102,7 @@
     kv = (cn_ref, k_ref, v_ref)
 
     def kv_copy(i, src, dst, sem, device):
-        return remote(kv[i].at[src], kv[i].at[dst], kv_send.at[sem, i], kv_recv.at[sem, i], device)
+        return remote(kv[i].at[src], kv[i].at[dst], kv_send.at[sem, i], kv_recv.at[sem, i], device, True)
 
     w_copies = []
 
@@ -105,13 +110,13 @@
         for j, w in enumerate((wg_hbm, wu_hbm)):
             w_copies.append(remote(
                 w.at[:, pl.ds(half * QUART, QUART)], wgu_ref.at[1, :, pl.ds((2 * half + j) * QUART, QUART)],
-                w_send.at[2 * half + j], w_recv.at[2 * half + j], mate,
+                w_send.at[2 * half + j], w_recv.at[2 * half + j], mate, True,
             ))
 
     below = [kv_copy(0, 2, 0, 0, prev_chip)]
     above = [kv_copy(0, 2, 4, 1, next_chip)]
     loads[0].wait()
-    q_copy = remote(qo_ref, q_ref, kv_send.at[4, 0], kv_recv.at[4, 0], prev_chip)
+    q_copy = remote(qo_ref, q_ref, kv_send.at[4, 0], kv_recv.at[4, 0], prev_chip, True)
     for i in (1, 2):
         loads[i].wait()
         below.append(kv_copy(i, 2, 0, 0, prev_chip))
@@ -161,25 +166,22 @@
         total = jnp.sum(expo, axis=-1, keepdims=True)
         vals = v_ref[:, :, cols].reshape((WMAX + 1) * TOK, HD)
         att = jnp.dot(expo.astype(jnp.bfloat16), vals, preferred_element_type=jnp.float32) / total
-        att_ref[:, cols] = att
+        nrm_ref[:, :, cols] = (att * gain_ref[cols].reshape(1, HD)).astype(jnp.bfloat16).reshape(2, HALF, HD)
         squares = squares + att * att
     row = jnp.broadcast_to(jnp.sum(squares, axis=1, keepdims=True), (TOK, TOK))
     ss_ref[0] = jnp.transpose(row)[0:8]
-    ss_copies = [
-        remote(ss_ref.at[0], ss_ref.at[j], ss_send.at[j], ss_recv.at[j], device)
-        for j, device in enumerate((y_h, *x_dev[1:], *xh_dev[1:]), start=1)
-    ]
-    for copy in ss_copies:
-        copy.wait_recv()
-    total = ss_ref[0]
-    for j in range(1, 8):
-        total = total + ss_ref[j]
-    factor = lax.rsqrt(total / D + 1e-06)
-    factor = jnp.transpose(jnp.broadcast_to(factor[0:1], (TOK, TOK)))
-    for h in range(WID // HD):
-        cols = pl.ds(h * HD, HD)
-        normed = (att_ref[:, cols] * factor * gain_ref[cols].reshape(1, HD)).astype(jnp.bfloat16)
-        nrm_ref[:, :, cols] = normed.reshape(2, HALF, HD)
+    for j, device in enumerate((y_h, *x_dev[1:], *xh_dev[1:], *yl_dev), start=1):
+        remote(ss_ref.at[0], ss_ref.at[j], ss_sem.at[0], ss_sem.at[1], device)
+
+    def norm_factors():
+        landed(ss_ref.at[pl.ds(1, 15)], ss_sem.at[1])
+        for group in range(2):
+            total = ss_ref[8 * group]
+            for j in range(1, 8):
+                total = total + ss_ref[8 * group + j]
+            factor = lax.rsqrt(total / D + 1e-06)
+            factor = jnp.transpose(jnp.broadcast_to(factor[0:1], (TOK, TOK)))
+            fac_ref[group] = factor.reshape(2, HALF, HD)
 
     y_copies = []
 
@@ -188,9 +190,9 @@
         rows = pl.ds(off, size)
         x_refs[i][SLOTS[i][0], 0, 0, 0] = nrm_ref[th, rows]
         y_copies.append([
-            remote(nrm_ref.at[1 - th, rows], x_refs[i].at[SLOTS[i][0], 0, 1, 0], y_sem.at[0, i, 0], y_sem.at[1, i, 0], mate),
-            remote(nrm_ref.at[th, rows], x_refs[i].at[SLOTS[i][0], 0, 0, 1], y_sem.at[0, i, 1], y_sem.at[1, i, 1], y_l),
-            remote(nrm_ref.at[1 - th, rows], x_refs[i].at[SLOTS[i][0], 0, 1, 1], y_sem.at[0, i, 2], y_sem.at[1, i, 2], mate_l),
+            remote(nrm_ref.at[1 - th, rows], x_refs[i].at[SLOTS[i][0], 0, 1, 0], out_sem.at[0, i], y_sem.at[i], mate),
+            remote(nrm_ref.at[th, rows], x_refs[i].at[SLOTS[i][0], 0, 0, 1], out_sem.at[0, i], y_sem.at[i], y_l),
+            remote(nrm_ref.at[1 - th, rows], x_refs[i].at[SLOTS[i][0], 0, 1, 1], out_sem.at[0, i], y_sem.at[i], mate_l),
         ])
 
     ring, relay = {}, {}
@@ -203,24 +205,36 @@
         if m == 4:
             src_ref, dst_ref = src_ref.at[way], dst_ref.at[way]
         ring[i, way, m] = remote(
-            src_ref, dst_ref, ag_sem.at[0, i, way, m - 1], ag_sem.at[1, i, way, m - 1], ups[way]
+            src_ref, dst_ref, out_sem.at[1, i], ag_sem.at[i, m - 1], ups[way]
         )
 
     def relay_send(i, slot):
         relay[i, slot] = remote(
-            x_refs[i].at[slot, 0], x_refs[i].at[slot, 1], rl_sem.at[0, i, slot], rl_sem.at[1, i, slot], core
+            x_refs[i].at[slot, 0], x_refs[i].at[slot, 1], out_sem.at[2, i], rl_sem.at[i, (slot + 1) // 2], core
         )
 
     def gather(i, m):
         if m == 0:
-            for copy in y_copies[i]:
-                copy.wait_recv()
+            landed(f_refs[i].at[1], y_sem.at[i])
+            off, size = SPLITS[i]
+            at = SLOTS[i][0]
+            for group in range(2):
+                factor = fac_ref[group, th, pl.ds(off, size)]
+                for half in range(2):
+                    for h in range(WID // HD):
+                        cols = pl.ds(h * HD, HD)
+                        x_refs[i][at, 0, half, group, :, cols] = (
+                            x_refs[i][at, 0, half, group, :, cols].astype(jnp.float32) * factor
+                        ).astype(jnp.bfloat16)
             ring_send(i, 0, 1)
             ring_send(i, 1, 1)
             relay_send(i, SLOTS[i][0])
             return
+        if m < 4:
+            landed(x_refs[i].at[pl.ds(0, 2), 0], ag_sem.at[i, m - 1])
+        else:
+            landed(x_refs[i].at[0, 0], ag_sem.at[i, m - 1])
         for way in range(2):
-            ring[i, way, m].wait_recv()
             if m < 4:
                 ring_send(i, way, m + 1)
                 relay_send(i, SLOTS[i][(-1, 1)[way] * m])
@@ -233,8 +247,7 @@
         slot, count = GROUPS[m]
         size = SPLITS[i][1]
         if way == 0:
-            for k in range(slot, slot + count):
-                relay[i, k].wait_recv()
+            landed(x_refs[i].at[pl.ds(slot, count), 1], rl_sem.at[i, m])
         for n in range(way * HID, (way + 1) * HID, 256):
             acc = None
             for half in range(2):
@@ -250,7 +263,7 @@
             ps_refs[i].at[slots, :, 1 - yh, :, pl.ds(HID, HID)],
         )[way]
         pa_copies[i, m, way] = remote(
-            out, pa_refs[i].at[slots, way], pa_sem.at[0, i, m, way], pa_sem.at[1, i, m, way], across[way]
+            out, pa_refs[i].at[slots, way], out_sem.at[3, i], pa_sem.at[i, m, way], across[way]
         )
 
     def combine(i, m, way):
@@ -266,7 +279,7 @@
             ).astype(jnp.bfloat16)
         p_copies[i, m, way] = remote(
             ps_refs[i].at[slots, a, b, :, cols], pr_refs[i].at[slots, way],
-            p_sem.at[0, i, m, way], p_sem.at[1, i, m, way], across[1 - way],
+            out_sem.at[4, i], p_sem.at[i, m, way], across[1 - way],
         )
 
     def hidden(i, m, way):
@@ -284,7 +297,7 @@
             h_refs[i][k, xa, yh, :, cols] = (gate / (1.0 + jnp.exp(-gate)) * up).astype(jnp.bfloat16)
         ref = h_refs[i].at[slots, xa, yh, :, cols]
         h_copies[i, m, way] = remote(
-            ref, ref, h_sem.at[0, i, m, way], h_sem.at[1, i, m, way], across[1 - way]
+            ref, ref, out_sem.at[5, i], h_sem.at[i, m, way], across[1 - way]
         )
 
     def forward(i, m, way):
@@ -294,14 +307,13 @@
         cols = pl.ds(way * QUART, QUART)
         ref = (h_refs[i].at[slots, xa, :, :, cols], h_refs[i].at[slots, :, yh, :, cols])[way]
         hf_copies[i, m, way] = remote(
-            ref, ref, hf_sem.at[0, i, m, way], hf_sem.at[1, i, m, way], across[way]
+            ref, ref, out_sem.at[6, i], hf_sem.at[i, m], across[way]
         )
 
     def down(i, m):
         slot, count = GROUPS[m]
         size = SPLITS[i][1]
-        for way in range(2):
-            hf_copies[i, m, way].wait_recv()
+        landed(h_refs[i].at[pl.ds(slot, count), 0], hf_sem.at[i, m])
         rows = h_refs[i][slot : slot + count].reshape(count * 4 * size, HID)
         for half in range(2):
             for n in range(0, WID, 256):
@@ -311,7 +323,7 @@
                 os_refs[i][slot : slot + count, half, :, :, n : n + 256] = o[:, 1].astype(jnp.bfloat16)
         o_copies[i, m] = remote(
             os_refs[i].at[pl.ds(slot, count)], oc_refs[i].at[pl.ds(slot, count)],
-            o_sem.at[0, i, m], o_sem.at[1, i, m], core,
+            out_sem.at[7, i], o_sem.at[i, m], core,
         )
 
     def both_cores(i, m):
@@ -324,13 +336,16 @@
         return 4 if offset == -3 else offset - 1
 
     def sums(i, r):
+        if r == 1:
+            landed(oc_refs[i].at[0], r_sem.at[i, 0])
+        elif r > 1:
+            landed(oc_refs[i].at[pl.ds(0, 2)], r_sem.at[i, r - 1])
         for way in range(2):
             sign = (1, -1)[way]
             if r == 0:
                 rs_refs[i][way, 0, 0] = oo_refs[i][SLOTS[i][3], way].astype(jnp.bfloat16)
                 src, dst = rs_refs[i].at[way, 0, 0], rr_refs[i].at[way, 0, way]
             else:
-                r_copies[i, way, r - 1].wait_recv()
                 slot = SLOTS[i][origin(sign * (4 - r))]
                 if r == 1:
                     rs_refs[i][way, 1, way] = (
@@ -342,27 +357,25 @@
                         oo_refs[i][slot] + rr_refs[i][way, r - 1].astype(jnp.float32)
                     ).astype(jnp.bfloat16)
                 src, dst = rs_refs[i].at[way, r], rr_refs[i].at[way, r]
-            r_copies[i, way, r] = remote(src, dst, r_sem.at[0, i, way, r], r_sem.at[1, i, way, r], ups[way])
+            r_copies[i, way, r] = remote(src, dst, out_sem.at[8, i], r_sem.at[i, r], ups[way])
 
     mine_at = 1 - (z + NZ - 1) // NZ
 
     def deliver(i):
-        for way in range(2):
-            r_copies[i, way, 3].wait_recv()
+        landed(oc_refs[i].at[pl.ds(0, 2)], r_sem.at[i, 3])
         ref, got, slot = oo_refs[i], rr_refs[i], SLOTS[i][-1]
         ref[slot] += got[0, 3].astype(jnp.float32) + got[1, 3].astype(jnp.float32)
         ref[slot, :, mine_at] += x_refs[i][slot, 0, :, mine_at].astype(jnp.float32)
         for j, (half, group, device) in enumerate(((0, 1 - mine_at, y_l), (1, mine_at, mate), (1, 1 - mine_at, mate_l))):
             f_refs[i][0, j] = ref[slot, half, group].astype(jnp.bfloat16)
             f_copies[i, j] = remote(
-                f_refs[i].at[0, j], f_refs[i].at[1, j], f_sem.at[0, i, j], f_sem.at[1, i, j], device
+                f_refs[i].at[0, j], f_refs[i].at[1, j], out_sem.at[9, i], f_sem.at[i], device
             )
 
     def finish(i):
         off, size = SPLITS[i]
         rows = pl.ds(off, size)
-        for j in range(3):
-            f_copies[i, j].wait_recv()
+        landed(f_refs[i].at[1], f_sem.at[i])
         got = f_refs[i]
         mine = oo_refs[i][SLOTS[i][-1], 0, mine_at] + got[1, 0].astype(jnp.float32)
         theirs = got[1, 1].astype(jnp.float32) + got[1, 2].astype(jnp.float32)
@@ -378,7 +391,7 @@
         for copy in w_copies[2 * half : 2 * half + 2]:
             copy.wait_recv()
         if half == 1:
-            w_copies.append(remote(wd_hbm, wd_ref.at[1], w_send.at[4], w_recv.at[4], mate))
+            w_copies.append(remote(wd_hbm, wd_ref.at[1], w_send.at[4], w_recv.at[4], mate, True))
 
     at(SECOND, 0, weights, 1)
     at(DOWN, 9, lambda: w_copies[4].wait_recv())
@@ -410,6 +423,7 @@
         copy.wait_send()
     sent[:] = [copy for copy in sent if all(copy is not old for old in w_copies)]
     send_weights(1)
+    norm_factors()
     gather(0, 0)
     early = [p for p in plan if p[1] == -1]
     for p in sorted(early):
@@ -422,6 +436,14 @@
 
     for copy in sent:
         copy.wait_send()
+    landed(ss_ref.at[pl.ds(1, 15)], ss_sem.at[0])
+    for i in range(len(SPLITS)):
+        blocks = oc_refs[i].at[pl.ds(0, 7)]
+        for j, ref in enumerate((
+            f_refs[i].at[0], blocks, x_refs[i].at[:, 0], pa_refs[i], pr_refs[i], h_refs[i].at[:, 0, 0],
+            h_refs[i].at[:, 0], os_refs[i], blocks, f_refs[i].at[0],
+        )):
+            landed(ref, out_sem.at[j, i])
 
 
 def per_device(queries, keys, values, window, counts, gain, w_gate, w_up, w_down):
@@ -441,8 +463,7 @@
         pltpu.VMEM((WMAX + 1, TOK, WID), bf),
         pltpu.VMEM((WMAX + 1, 8, 128), jnp.int32),
         pltpu.VMEM((WID // HD, TOK, (WMAX + 1) * TOK), f32),
-        pltpu.VMEM((TOK, WID), f32),
-        pltpu.VMEM((8, 8, 128), f32),
+        pltpu.VMEM((16, 8, 128), f32),
         pltpu.VMEM((2, HALF, WID), bf),
         pltpu.VMEM((2, WID, 2 * HID), bf),
         pltpu.VMEM((2, HID, WID), bf),
@@ -457,10 +478,10 @@
         each(lambda s: (2, 4, 2, 2, s, WID), bf),
         each(lambda s: (2, 4, 2, 2, s, WID), bf),
         each(lambda s: (2, 3, s, WID), bf),
-        dma((8,)), dma((5, 3)), dma((5, 3)), dma((5,)), dma((5,)), dma((8,)), dma((8,)),
-        dma((2, n, 3)), dma((2, n, 2, 4)), dma((2, n, NZ)), dma((2, n, steps, 2)), dma((2, n, steps, 2)),
-        dma((2, n, steps, 2)), dma((2, n, steps, 2)),
-        dma((2, n, steps)), dma((2, n, 2, 4)), dma((2, n, 3)),
+        dma((8,)), dma((5, 3)), dma((5, 3)), dma((5,)), dma((5,)), dma((2,)), dma((10, n)),
+        pltpu.VMEM((2, 2, HALF, HD), f32),
+        dma((n,)), dma((n, 4)), dma((n, steps)), dma((n, steps, 2)), dma((n, steps, 2)), dma((n, steps, 2)),
+        dma((n, steps)), dma((n, steps)), dma((n, 4)), dma((n,)),
     ]
     hbm = pl.BlockSpec(memory_space=pl.ANY)
     smem = pl.BlockSpec(memory_space=pltpu.SMEM)

time: 141 us -> 134 us (0.950)
  Pallas kernels: 138 us -> 131 us
    pallas_call x1, Pallas kernels: 138 us -> 131 us  [per_device(): pl.pallas_call(body, out_shape=jax.ShapeDtypeStruct((2, HALF, WID), bf),...]
where the time goes in v4:
time: 134 us
  Pallas kernels  131 us (98%)
  local copies, waits for them, and re-layouts  1.62 us (1%)
    pallas_call x1, Pallas kernels, per_device(): pl.pallas_call(body, out_shape=jax.ShapeDtypeStruct((2, HALF, WID), bf),...  131 us

profile of v4, /device:TPU:1, one launch (start us, length us, event | category | flops | bytes accessed | tf_op | source)
XLA Modules:
  0.0 134.4 jit_solution(4813816285597632187)
XLA Ops:
  1.3 131.4 %block.1 = bf16[2,64,768]{2,1,0:T(8,128)(2,1)} custom-call(bf16[128,768]{1,0:T(8,128)(2,1)} %q_hbm.1, bf16[128,768]{1,0:T(8,128)(2,1)} %k_hbm.1, bf16[128,768]{1,0:T(8,128)(2,1)} %v_hbm.1, s32[1]{0:T(128)S(6)} %copy.11.win_ref, s32[1]{0:T(128)S(6)} %copy.12.cnt_ref, f32[768]{0:T(1024)} %gain_ref.1, bf16[768,512]{1,0:T(8,128)(2,1)} %wg_hbm.1, ...), custom_call_target="tpu_custom_call" | custom-call | flops 10000000000 | bytes 3000000 | tf_op jit(solution)/shard_map/block/pallas_call | solution.py:489
  132.7 1.6 %copy.13 = bf16[128,768]{1,0:T(8,128)(2,1)} copy(bf16[128,768]{1,0:T(8,128)(2,1)} %bitcast.1) | data formatting | bytes 393216

commit v5 on v4

--- a/solution.py
+++ b/solution.py
@@ -119,7 +119,8 @@
     q_copy = remote(qo_ref, q_ref, kv_send.at[4, 0], kv_recv.at[4, 0], prev_chip, True)
     for i in (1, 2):
         loads[i].wait()
-        below.append(kv_copy(i, 2, 0, 0, prev_chip))
+        if i == 1:
+            below.append(kv_copy(i, 2, 0, 0, prev_chip))
         above.append(kv_copy(i, 2, 4, 1, next_chip))
     send_weights(0)
 
@@ -139,24 +140,27 @@
             s_ref[h, :, pl.ds(e * TOK, TOK)] = jnp.where(visible, s, -1e30)
 
     q_copy.wait_recv()
+    below.append(kv_copy(2, 2, 0, 0, prev_chip))
     below[0].wait_recv()
+    near = [kv_copy(0, 2 * c, 1, 2, core)]
     score(2)
-    near, mid = [], []
+    mid = []
     for i in range(3):
         above[i].wait_recv()
         mid.append(kv_copy(i, 2 * c + 2, 3, 3, core))
     score(4)
-    for i in range(3):
-        if i > 0:
-            below[i].wait_recv()
-        near.append(kv_copy(i, 2 * c, 1, 2, core))
+    below[1].wait_recv()
+    near.append(kv_copy(1, 2 * c, 1, 2, core))
     score(0)
     for i in range(3):
         mid[i].wait_recv()
     score(3)
-    for i in range(3):
+    for i in range(2):
         near[i].wait_recv()
     score(1)
+    below[2].wait_recv()
+    near.append(kv_copy(2, 2 * c, 1, 2, core))
+    near[2].wait_recv()
 
     squares = jnp.zeros((TOK, HD), jnp.float32)
     for h in range(WID // HD):

time: 134 us -> 134 us (level)
  no operation moved by 1% of the time
where the time goes in v5:
time: 134 us
  Pallas kernels  131 us (98%)
  local copies, waits for them, and re-layouts  1.62 us (1%)
    pallas_call x1, Pallas kernels, per_device(): pl.pallas_call(body, out_shape=jax.ShapeDtypeStruct((2, HALF, WID), bf),...  131 us

profile of v5, /device:TPU:1, one launch (start us, length us, event | category | flops | bytes accessed | tf_op | source)
XLA Modules:
  0.0 134.1 jit_solution(16159918929364218691)
XLA Ops:
  1.3 131.1 %block.1 = bf16[2,64,768]{2,1,0:T(8,128)(2,1)} custom-call(bf16[128,768]{1,0:T(8,128)(2,1)} %q_hbm.1, bf16[128,768]{1,0:T(8,128)(2,1)} %k_hbm.1, bf16[128,768]{1,0:T(8,128)(2,1)} %v_hbm.1, s32[1]{0:T(128)S(6)} %copy.11.win_ref, s32[1]{0:T(128)S(6)} %copy.12.cnt_ref, f32[768]{0:T(1024)} %gain_ref.1, bf16[768,512]{1,0:T(8,128)(2,1)} %wg_hbm.1, ...), custom_call_target="tpu_custom_call" | custom-call | flops 10000000000 | bytes 3000000 | tf_op jit(solution)/shard_map/block/pallas_call | solution.py:493
  132.4 1.6 %copy.13 = bf16[128,768]{1,0:T(8,128)(2,1)} copy(bf16[128,768]{1,0:T(8,128)(2,1)} %bitcast.1) | data formatting | bytes 393216

commit v6 on v4

--- a/solution.py
+++ b/solution.py
@@ -25,10 +25,10 @@
 GROUPS = ((0, 1), (1, 2), (3, 2), (5, 2), (7, 1))
 STEPS = tuple((i, m) for m in range(5) for i in (0, 1)) + tuple((i, 4 - m) for m in range(5) for i in (2, 3))
 LAGS = (0, 1, 2, 3, 4, 5)
-GATHERS = ((None, 1, 3, 5, 6), (-13, 2, 4, 6, 7), (-10, 5, 6, 8, 10), (3, 5, 7, 9, 10))
-EARLY = 0
+GATHERS = ((None, 0, 3, 4, 6), (-2, 2, 4, 6, 7), (-21, 5, 7, 8, 10), (3, 5, 7, 10, 12))
+EARLY = -1
 SECOND, DOWN = 6, 10
-HOLD = ((2, 2, 2, 1, 5, 4), (0, 2, 2, 2, 4, 2), (0, 1, 1, 0, 1, 7), (0, 1, 0, 0, 4, 5))
+HOLD = ((0, 3, 3, 3, 5, 9), (0, 1, 6, 3, 14, 11), (0, 0, 0, 0, 6, 10), (0, 0, 0, 0, 15, 7))
 
 
 def body(

time: 134 us -> 134 us (level)
  no operation moved by 1% of the time
where the time goes in v6:
time: 134 us
  Pallas kernels  131 us (98%)
  local copies, waits for them, and re-layouts  1.62 us (1%)
    pallas_call x1, Pallas kernels, per_device(): pl.pallas_call(body, out_shape=jax.ShapeDtypeStruct((2, HALF, WID), bf),...  131 us

profile of v6, /device:TPU:1, one launch (start us, length us, event | category | flops | bytes accessed | tf_op | source)
XLA Modules:
  0.0 134.2 jit_solution(7635701524843079843)
XLA Ops:
  1.3 131.3 %block.1 = bf16[2,64,768]{2,1,0:T(8,128)(2,1)} custom-call(bf16[128,768]{1,0:T(8,128)(2,1)} %q_hbm.1, bf16[128,768]{1,0:T(8,128)(2,1)} %k_hbm.1, bf16[128,768]{1,0:T(8,128)(2,1)} %v_hbm.1, s32[1]{0:T(128)S(6)} %copy.11.win_ref, s32[1]{0:T(128)S(6)} %copy.12.cnt_ref, f32[768]{0:T(1024)} %gain_ref.1, bf16[768,512]{1,0:T(8,128)(2,1)} %wg_hbm.1, ...), custom_call_target="tpu_custom_call" | custom-call | flops 10000000000 | bytes 3000000 | tf_op jit(solution)/shard_map/block/pallas_call | solution.py:489
  132.6 1.6 %copy.13 = bf16[128,768]{1,0:T(8,128)(2,1)} copy(bf16[128,768]{1,0:T(8,128)(2,1)} %bitcast.1) | data formatting | bytes 393216
